TPU v7x, 32 devices: a whole 2x2x4 slice. The times are simulated.
32 devices in a mesh: slab: 8 (over y, x, core), pencil: 4 (over z).
Axes of the slice: x: 2, y: 2, z: 4, core: 2. Of those that a mesh axis runs over, the one named last changes fastest.
Arguments:
- cotangent: float32 [32, 512, 512], P('slab', 'pencil'), may hold values from -6 to 6
- seg_rows: int32 [32, 4], replicated, may hold values from 1 to 64, 128 in all within a row
- owners: int32 [32, 4], replicated, may hold values from 0 to 31
- offsets: int32 [32, 4], replicated, may hold values from 0 to 64
Outputs:
- rhs_grad: float32 [32, 512, 512], P('slab', 'pencil')
- parent_grad: float32 [32, 128, 128], P(('slab', 'pencil'))
Inputs may be any that keep to these rules, and one draw needn't show every extreme that they name: `seg_rows`: each tile's 4 row counts sum to 128; in every tile one segment has exactly 64 rows.
All inputs are finite; a program needn't handle non-finite values.
Results may differ from a plain program's by a relative error of at most 0.00002.
Values sent between devices are 32-bit elements; how exact they have to be, the bound alone decides.
A program may use at most 192 MiB of HBM per device.

v0:
```python
import jax
import jax.numpy as jnp
from jax import lax
from jax.sharding import PartitionSpec as P

TILE = 128
PT_DEV = 1


omega_weight = 2.0 / 3.0


def with_halo(x, sides, width):
    for axis, dim in sides:
        peers, length = (lax.axis_size(axis), x.shape[dim])
        up = [(i, (i + 1) % peers) for i in range(peers - 1)]
        down = [(j, i) for i, j in up]
        last = lax.slice_in_dim(x, length - width, length, axis=dim)
        initial = lax.slice_in_dim(x, 0, width, axis=dim)
        before = lax.ppermute(last, axis, up)
        after = lax.ppermute(initial, axis, down)
        x = jnp.concatenate([before, x, after], axis=dim)
    return x


def neighbour_sum(padded):
    total = padded[2:, 1:-1, 1:-1] + padded[:-2, 1:-1, 1:-1]
    total = total + padded[1:-1, 2:, 1:-1] + padded[1:-1, :-2, 1:-1]
    total = total + padded[1:-1, 1:-1, 2:] + padded[1:-1, 1:-1, :-2]
    return total


def block_neighbours(field):
    padded = with_halo(field, (("slab", 0), ("pencil", 1)), 1)
    return neighbour_sum(jnp.pad(padded, ((0, 0), (0, 0), (1, 1))))


def coarse_neighbours(field):
    padded = with_halo(field, (("slab", 0), ("pencil", 1)), 1)
    return neighbour_sum(jnp.pad(padded, ((0, 0), (0, 0), (1, 1))))


def coefficient(level):
    return omega_weight * 4.0**level / 6.0


def smoothed(field, neighbours):
    return (1.0 - omega_weight) * field + omega_weight / 6.0 * neighbours


def children_sum(field):
    x_cells, y_cells, z_cells = field.shape
    blocks = field.reshape(x_cells // 2, 2, y_cells // 2, 2, z_cells // 2, 2)
    return jnp.sum(blocks, axis=(1, 3, 5))


def prolong(field):
    return jnp.repeat(jnp.repeat(jnp.repeat(field, 2, axis=0), 2, axis=1), 2, axis=2)


def source_rows(seg_rows, owners, offsets, tile_size):
    starts = jnp.cumsum(seg_rows, axis=1) - seg_rows
    position = jnp.arange(tile_size, dtype=jnp.int32)[None, None, :]
    inside = (position >= starts[:, :, None]) & (position < (starts + seg_rows)[:, :, None])
    value = owners[:, :, None] * tile_size + offsets[:, :, None] + position - starts[:, :, None]
    return jnp.sum(jnp.where(inside, value, 0), axis=1)


def tile_rows(faces, tile_size):
    face_count, y_cells, z_cells = faces.shape
    blocks = faces.reshape(
        face_count, y_cells // tile_size, tile_size, z_cells // tile_size, tile_size
    )
    return blocks.transpose(0, 1, 3, 2, 4).reshape(-1, tile_size)


def add_rows(rows_data, targets, first_row, slot_count):
    shifted = targets - first_row
    segment_ids = jnp.where((shifted >= 0) & (shifted < slot_count), shifted, slot_count)
    summed = jax.ops.segment_sum(rows_data, segment_ids, num_segments=slot_count + 1)
    return summed[:slot_count]


def shards(cotangent, seg_rows, owners, offsets):
    x_cells, y_cells, z_cells = cotangent.shape
    tile_size = TILE
    grad_fine = cotangent
    rhs_grad = jnp.zeros_like(cotangent)
    for sweep_number in range(3):
        rhs_grad = rhs_grad + coefficient(0) * grad_fine
        grad_fine = smoothed(grad_fine, block_neighbours(grad_fine))
    medium = children_sum(grad_fine)
    grad_medium = jnp.zeros_like(medium)
    for sweep_number in range(3):
        grad_medium = grad_medium + coefficient(1) * medium
        medium = smoothed(medium, block_neighbours(medium))
    coarse_cot = children_sum(medium)
    grad_coarse = coefficient(2) * coarse_cot
    for sweep_number in range(2):
        coarse_cot = smoothed(coarse_cot, coarse_neighbours(coarse_cot))
        grad_coarse = grad_coarse + coefficient(2) * coarse_cot
    back_medium = prolong(grad_coarse) * 0.125
    grad_medium = grad_medium + back_medium
    medium = medium - (6.0 * back_medium - block_neighbours(back_medium)) / 4.0
    for sweep_number in range(3):
        grad_medium = grad_medium + coefficient(1) * medium
        if sweep_number < 2:
            medium = smoothed(medium, block_neighbours(medium))
    back_fine = prolong(grad_medium) * 0.125
    rhs_grad = rhs_grad + back_fine
    grad_fine = grad_fine - (6.0 * back_fine - block_neighbours(back_fine))
    for sweep_number in range(3):
        rhs_grad = rhs_grad + coefficient(0) * grad_fine
        if sweep_number < 2:
            grad_fine = smoothed(grad_fine, block_neighbours(grad_fine))
    slab_index = lax.axis_index("slab")
    slab_count = lax.axis_size("slab")
    low_part = jnp.where(slab_index == 0, rhs_grad[0], 0.0)
    high_part = jnp.where(slab_index == slab_count - 1, rhs_grad[x_cells - 1], 0.0)
    summed_faces = lax.psum(jnp.stack([low_part, high_part]), "slab")
    all_faces = lax.all_gather(summed_faces, "pencil", axis=1, tiled=True)
    all_rows = tile_rows(all_faces, tile_size)
    targets = source_rows(seg_rows, owners, offsets, tile_size)
    first_row = lax.axis_index(("slab", "pencil")) * (PT_DEV * tile_size)
    owned = add_rows(all_rows, targets.reshape(-1), first_row, PT_DEV * tile_size)
    parent_grad = owned.reshape(PT_DEV, tile_size, tile_size)
    return (rhs_grad, parent_grad)


def solution(mesh):
    return jax.shard_map(
        shards,
        mesh=mesh,
        in_specs=(P("slab", "pencil", None), P(), P(), P()),
        out_specs=(P("slab", "pencil", None), P(("slab", "pencil"), None, None)),
        check_vma=False,
    )
```

profile of v0, /device:TPU:0, one launch (start us, length us, event | category | flops | bytes accessed | tf_op | source)
XLA Modules:
  0.0 615.0 jit_solution(14866246169576770804)
XLA Ops:
  21.6 5.6 collective-permute-start.3
  37.8 5.1 collective-permute-start.5
  51.4 4.5 collective-permute-start.7
  66.4 8.3 %collective-permute-start.9 = (f32[1,128,512]{1,2,0:T(8,128)S(1)}, f32[1,128,512]{1,2,0:T(8,128)S(1)}, u32[]{:S(2)}, u32[]{:S(2)}) collective-permute-start(f32[1,128,512]{1,2,0:T(8,128)S(1)} %get-tuple-element.34), channel_id=1, source_target_pairs={{0,4},{4,8},{8,12},{12,16},{16,20},{20,24},{24,28},{1,5},{5,9},{9,... | collective-permute-start | bytes 786440 | tf_op jit(solution)/shard_map/ppermute | solution.py:20
  83.9 4.7 collective-permute-start.11
  100.4 69.2 %reshape.120 = f32[2,2,64,2,256,2]{5,4,3,2,1,0:T(8,128)} reshape(f32[4,128,512]{2,1,0:T(8,128)} %copy.138) | data formatting | bytes 2097152 | tf_op jit(solution)/shard_map/reshape | solution.py:53
  169.5 20.8 %reduce_sum.36 = f32[2,64,256]{2,1,0:T(8,128)S(1)} reduce(f32[2,2,64,2,256,2]{5,4,3,2,1,0:T(8,128)} %reshape.120, f32[]{:T(128)} %constant.17.clone.1), dimensions={1,3,5}, to_apply=%region_0.1 | reduce | flops 229376 | bytes 1179652 | tf_op jit(solution)/shard_map/reduce_sum | solution.py:54
  191.6 7.2 %collective-permute-start.13 = (f32[1,64,256]{2,1,0:T(8,128)S(1)}, f32[1,64,256]{2,1,0:T(8,128)S(1)}, u32[]{:S(2)}, u32[]{:S(2)}) collective-permute-start(f32[1,64,256]{2,1,0:T(8,128)S(1)} %get-tuple-element.62), channel_id=1, source_target_pairs={{0,4},{4,8},{8,12},{12,16},{16,20},{20,24},{24,28},{1,5},{5,9},{9,... | collective-permute-start | bytes 196616 | tf_op jit(solution)/shard_map/ppermute | solution.py:20
  201.0 4.5 collective-permute-start.15
  208.5 4.9 collective-permute-start.17
  215.6 4.5 collective-permute-start.19
  223.1 5.6 collective-permute-start.21
  238.4 6.3 %reduce_sum.38 = f32[32,2,128,2]{3,2,1,0:T(8,128)} reshape(f32[64,256]{1,0:T(8,128)} %get-tuple-element.14) | data formatting | bytes 131072 | tf_op jit(solution)/shard_map/reduce_sum | solution.py:54
  248.7 5.6 collective-permute-start.25
  256.5 4.5 collective-permute-start.27
  263.8 5.2 collective-permute-start.29
  271.1 4.5 collective-permute-start.31
  282.7 6.9 %collective-permute-start.33 = (f32[1,64,256]{1,2,0:T(8,128)}, f32[1,64,256]{1,2,0:T(8,128)}, u32[]{:S(2)}, u32[]{:S(2)}) collective-permute-start(f32[1,64,256]{1,2,0:T(8,128)} %bitcast.7), channel_id=1, source_target_pairs={{0,4},{4,8},{8,12},{12,16},{16,20},{20,24},{24,28},{1,5},{5,9},{9,... | collective-permute-start | bytes 196616 | tf_op jit(solution)/shard_map/ppermute | solution.py:20
  298.0 4.5 collective-permute-start.35
  312.3 6.0 collective-permute-start.37
  320.5 4.6 collective-permute-start.39
  328.0 5.6 collective-permute-start.41
  335.8 4.8 collective-permute-start.43
  349.8 7.5 %collective-permute-start.45 = (f32[1,128,512]{1,2,0:T(8,128)}, f32[1,128,512]{1,2,0:T(8,128)}, u32[]{:S(2)}, u32[]{:S(2)}) collective-permute-start(f32[1,128,512]{1,2,0:T(8,128)} %bitcast.16), channel_id=1, source_target_pairs={{0,4},{4,8},{8,12},{12,16},{16,20},{20,24},{24,28},{1,5},{5,9},{9,... | collective-permute-start | bytes 786440 | tf_op jit(solution)/shard_map/ppermute | solution.py:20
  371.8 5.1 collective-permute-start.47
  396.2 5.1 collective-permute-start.49
  410.4 4.8 collective-permute-start.51
  425.1 7.3 %collective-permute-start.53 = (f32[1,128,512]{1,2,0:T(8,128)S(1)}, f32[1,128,512]{1,2,0:T(8,128)S(1)}, u32[]{:S(2)}, u32[]{:S(2)}) collective-permute-start(f32[1,128,512]{1,2,0:T(8,128)S(1)} %get-tuple-element.30), channel_id=1, source_target_pairs={{0,4},{4,8},{8,12},{12,16},{16,20},{20,24},{24,28},{1,5},{5,9},{9,... | collective-permute-start | bytes 786440 | tf_op jit(solution)/shard_map/ppermute | solution.py:20
  441.5 4.8 collective-permute-start.55
  457.8 69.6 %all-reduce.16.cloned.1.call-done = f32[2,128,512]{1,2,0:T(8,128)} async-done(((f32[2,128,512]{1,2,0:T(8,128)}), f32[2,128,512]{1,2,0:T(8,128)}) %all-reduce.16.cloned.1.call-update) | async-done | bytes 524304 | tf_op jit(solution)/shard_map/psum | solution.py:120
  530.2 44.4 %all-gather.2.cloned.1.call-done = f32[2,512,512]{1,2,0:T(8,128)} async-done(((f32[2,128,512]{1,2,0:T(8,128)}), f32[2,512,512]{1,2,0:T(8,128)}) %all-gather.2.cloned.1.call-update) | async-done | bytes 2097168 | tf_op jit(solution)/shard_map/all_gather | solution.py:121
  578.4 28.7 %scatter_custom_fusion = f32[129,128]{1,0:T(8,128)S(1)} fusion(s32[4096]{0:T(1024)S(1)} %bitcast.53, f32[4096,128]{1,0:T(8,128)} %bitcast.39, f32[]{:T(128)} %constant.17.clone.1), kind=kCustom, calls=%fused_computation.276 | custom fusion | flops 524288 | bytes 66560 | tf_op jit(solution)/shard_map/scatter-add | solution.py:80
  (294 shorter events, 218.4 us)
Async XLA Ops:
  7.2 520.2 %all-reduce.16.cloned.1.call-start = ((), (), s32[]{:S(2)}) async-start(), calls=%async_computation | async-start | bytes 1048576 | tf_op jit(solution)/shard_map/psum | solution.py:120
  18.4 8.7 %collective-permute-start.2 = (f32[6,1,512]{2,1,0:T(1,128)S(1)}, f32[6,1,512]{2,1,0:T(1,128)S(1)}, u32[]{:S(2)}, u32[]{:S(2)}) collective-permute-start(f32[6,1,512]{2,1,0:T(1,128)S(1)} %copy.119), channel_id=1, source_target_pairs={{1,0},{2,1},{3,2},{5,4},{6,5},{7,6},{9,8},{10,9},{11,10},{13,12},{... | collective-permute-start | bytes 36872 | tf_op jit(solution)/shard_map/ppermute | solution.py:21
  21.6 7.0 %collective-permute-start.3 = (f32[6,1,512]{2,1,0:T(1,128)S(1)}, f32[6,1,512]{2,1,0:T(1,128)S(1)}, u32[]{:S(2)}, u32[]{:S(2)}) collective-permute-start(f32[6,1,512]{2,1,0:T(1,128)S(1)} %copy.121), channel_id=1, source_target_pairs={{0,1},{1,2},{2,3},{4,5},{5,6},{6,7},{8,9},{9,10},{10,11},{12,13},{... | collective-permute-start | bytes 36872 | tf_op jit(solution)/shard_map/ppermute | solution.py:20
  48.2 7.7 %collective-permute-start.6 = (f32[6,1,512]{2,1,0:T(1,128)S(1)}, f32[6,1,512]{2,1,0:T(1,128)S(1)}, u32[]{:S(2)}, u32[]{:S(2)}) collective-permute-start(f32[6,1,512]{2,1,0:T(1,128)S(1)} %copy.126), channel_id=1, source_target_pairs={{1,0},{2,1},{3,2},{5,4},{6,5},{7,6},{9,8},{10,9},{11,10},{13,12},{... | collective-permute-start | bytes 36872 | tf_op jit(solution)/shard_map/ppermute | solution.py:21
  65.1 9.6 %collective-permute-start.8 = (f32[1,128,512]{1,2,0:T(8,128)S(1)}, f32[1,128,512]{1,2,0:T(8,128)S(1)}, u32[]{:S(2)}, u32[]{:S(2)}) collective-permute-start(f32[1,128,512]{1,2,0:T(8,128)S(1)} %get-tuple-element.35), channel_id=1, source_target_pairs={{4,0},{8,4},{12,8},{16,12},{20,16},{24,20},{28,24},{5,1},{9,5},{13... | collective-permute-start | bytes 786440 | tf_op jit(solution)/shard_map/ppermute | solution.py:21
  66.4 9.4 %collective-permute-start.9 = (f32[1,128,512]{1,2,0:T(8,128)S(1)}, f32[1,128,512]{1,2,0:T(8,128)S(1)}, u32[]{:S(2)}, u32[]{:S(2)}) collective-permute-start(f32[1,128,512]{1,2,0:T(8,128)S(1)} %get-tuple-element.34), channel_id=1, source_target_pairs={{0,4},{4,8},{8,12},{12,16},{16,20},{20,24},{24,28},{1,5},{5,9},{9,... | collective-permute-start | bytes 786440 | tf_op jit(solution)/shard_map/ppermute | solution.py:20
  80.7 7.9 %collective-permute-start.10 = (f32[6,1,512]{2,1,0:T(1,128)S(1)}, f32[6,1,512]{2,1,0:T(1,128)S(1)}, u32[]{:S(2)}, u32[]{:S(2)}) collective-permute-start(f32[6,1,512]{2,1,0:T(1,128)S(1)} %copy.132), channel_id=1, source_target_pairs={{1,0},{2,1},{3,2},{5,4},{6,5},{7,6},{9,8},{10,9},{11,10},{13,12},{... | collective-permute-start | bytes 36872 | tf_op jit(solution)/shard_map/ppermute | solution.py:21
  190.3 8.5 %collective-permute-start.12 = (f32[1,64,256]{2,1,0:T(8,128)S(1)}, f32[1,64,256]{2,1,0:T(8,128)S(1)}, u32[]{:S(2)}, u32[]{:S(2)}) collective-permute-start(f32[1,64,256]{2,1,0:T(8,128)S(1)} %get-tuple-element.63), channel_id=1, source_target_pairs={{4,0},{8,4},{12,8},{16,12},{20,16},{24,20},{28,24},{5,1},{9,5},{13... | collective-permute-start | bytes 196616 | tf_op jit(solution)/shard_map/ppermute | solution.py:21
  191.6 8.1 %collective-permute-start.13 = (f32[1,64,256]{2,1,0:T(8,128)S(1)}, f32[1,64,256]{2,1,0:T(8,128)S(1)}, u32[]{:S(2)}, u32[]{:S(2)}) collective-permute-start(f32[1,64,256]{2,1,0:T(8,128)S(1)} %get-tuple-element.62), channel_id=1, source_target_pairs={{0,4},{4,8},{8,12},{12,16},{16,20},{20,24},{24,28},{1,5},{5,9},{9,... | collective-permute-start | bytes 196616 | tf_op jit(solution)/shard_map/ppermute | solution.py:20
  221.8 6.9 %collective-permute-start.20 = (f32[1,64,256]{2,1,0:T(8,128)S(1)}, f32[1,64,256]{2,1,0:T(8,128)S(1)}, u32[]{:S(2)}, u32[]{:S(2)}) collective-permute-start(f32[1,64,256]{2,1,0:T(8,128)S(1)} %get-tuple-element.59), channel_id=1, source_target_pairs={{4,0},{8,4},{12,8},{16,12},{20,16},{24,20},{28,24},{5,1},{9,5},{13... | collective-permute-start | bytes 196616 | tf_op jit(solution)/shard_map/ppermute | solution.py:21
  223.1 6.5 %collective-permute-start.21 = (f32[1,64,256]{2,1,0:T(8,128)S(1)}, f32[1,64,256]{2,1,0:T(8,128)S(1)}, u32[]{:S(2)}, u32[]{:S(2)}) collective-permute-start(f32[1,64,256]{2,1,0:T(8,128)S(1)} %get-tuple-element.58), channel_id=1, source_target_pairs={{0,4},{4,8},{8,12},{12,16},{16,20},{20,24},{24,28},{1,5},{5,9},{9,... | collective-permute-start | bytes 196616 | tf_op jit(solution)/shard_map/ppermute | solution.py:20
  247.4 6.9 %collective-permute-start.24 = (f32[1,32,128]{2,1,0:T(8,128)S(1)}, f32[1,32,128]{2,1,0:T(8,128)S(1)}, u32[]{:S(2)}, u32[]{:S(2)}) collective-permute-start(f32[1,32,128]{2,1,0:T(8,128)S(1)} %bitcast.45), channel_id=1, source_target_pairs={{4,0},{8,4},{12,8},{16,12},{20,16},{24,20},{28,24},{5,1},{9,5},{13... | collective-permute-start | bytes 49160 | tf_op jit(solution)/shard_map/ppermute | solution.py:21
  262.5 6.5 %collective-permute-start.28 = (f32[1,32,128]{2,1,0:T(8,128)S(1)}, f32[1,32,128]{2,1,0:T(8,128)S(1)}, u32[]{:S(2)}, u32[]{:S(2)}) collective-permute-start(f32[1,32,128]{2,1,0:T(8,128)S(1)} %fusion.81), channel_id=1, source_target_pairs={{4,0},{8,4},{12,8},{16,12},{20,16},{24,20},{28,24},{5,1},{9,5},{13... | collective-permute-start | bytes 49160 | tf_op jit(solution)/shard_map/ppermute | solution.py:21
  281.4 9.8 %collective-permute-start.32 = (f32[1,64,256]{1,2,0:T(8,128)}, f32[1,64,256]{1,2,0:T(8,128)}, u32[]{:S(2)}, u32[]{:S(2)}) collective-permute-start(f32[1,64,256]{1,2,0:T(8,128)} %bitcast.7), channel_id=1, source_target_pairs={{4,0},{8,4},{12,8},{16,12},{20,16},{24,20},{28,24},{5,1},{9,5},{13... | collective-permute-start | bytes 196616 | tf_op jit(solution)/shard_map/ppermute | solution.py:21
  282.7 10.1 %collective-permute-start.33 = (f32[1,64,256]{1,2,0:T(8,128)}, f32[1,64,256]{1,2,0:T(8,128)}, u32[]{:S(2)}, u32[]{:S(2)}) collective-permute-start(f32[1,64,256]{1,2,0:T(8,128)} %bitcast.7), channel_id=1, source_target_pairs={{0,4},{4,8},{8,12},{12,16},{16,20},{20,24},{24,28},{1,5},{5,9},{9,... | collective-permute-start | bytes 196616 | tf_op jit(solution)/shard_map/ppermute | solution.py:20
  296.7 11.8 %collective-permute-start.34 = (f32[4,1,256]{2,1,0:T(1,128)S(1)}, f32[4,1,256]{2,1,0:T(1,128)S(1)}, u32[]{:S(2)}, u32[]{:S(2)}) collective-permute-start(f32[4,1,256]{2,1,0:T(1,128)S(1)} %get-tuple-element.47), channel_id=1, source_target_pairs={{1,0},{2,1},{3,2},{5,4},{6,5},{7,6},{9,8},{10,9},{11,10},{13,12},{... | collective-permute-start | bytes 12296 | tf_op jit(solution)/shard_map/ppermute | solution.py:21
  298.0 10.5 %collective-permute-start.35 = (f32[4,1,256]{2,1,0:T(1,128)S(1)}, f32[4,1,256]{2,1,0:T(1,128)S(1)}, u32[]{:S(2)}, u32[]{:S(2)}) collective-permute-start(f32[4,1,256]{2,1,0:T(1,128)S(1)} %get-tuple-element.46), channel_id=1, source_target_pairs={{0,1},{1,2},{2,3},{4,5},{5,6},{6,7},{8,9},{9,10},{10,11},{12,13},{... | collective-permute-start | bytes 12296 | tf_op jit(solution)/shard_map/ppermute | solution.py:20
  311.0 7.3 %collective-permute-start.36 = (f32[1,64,256]{2,1,0:T(8,128)S(1)}, f32[1,64,256]{2,1,0:T(8,128)S(1)}, u32[]{:S(2)}, u32[]{:S(2)}) collective-permute-start(f32[1,64,256]{2,1,0:T(8,128)S(1)} %get-tuple-element.57), channel_id=1, source_target_pairs={{4,0},{8,4},{12,8},{16,12},{20,16},{24,20},{28,24},{5,1},{9,5},{13... | collective-permute-start | bytes 196616 | tf_op jit(solution)/shard_map/ppermute | solution.py:21
  312.3 6.9 %collective-permute-start.37 = (f32[1,64,256]{2,1,0:T(8,128)S(1)}, f32[1,64,256]{2,1,0:T(8,128)S(1)}, u32[]{:S(2)}, u32[]{:S(2)}) collective-permute-start(f32[1,64,256]{2,1,0:T(8,128)S(1)} %get-tuple-element.56), channel_id=1, source_target_pairs={{0,4},{4,8},{8,12},{12,16},{16,20},{20,24},{24,28},{1,5},{5,9},{9,... | collective-permute-start | bytes 196616 | tf_op jit(solution)/shard_map/ppermute | solution.py:20
  326.7 6.9 %collective-permute-start.40 = (f32[1,64,256]{2,1,0:T(8,128)S(1)}, f32[1,64,256]{2,1,0:T(8,128)S(1)}, u32[]{:S(2)}, u32[]{:S(2)}) collective-permute-start(f32[1,64,256]{2,1,0:T(8,128)S(1)} %get-tuple-element.55), channel_id=1, source_target_pairs={{4,0},{8,4},{12,8},{16,12},{20,16},{24,20},{28,24},{5,1},{9,5},{13... | collective-permute-start | bytes 196616 | tf_op jit(solution)/shard_map/ppermute | solution.py:21
  328.0 6.5 %collective-permute-start.41 = (f32[1,64,256]{2,1,0:T(8,128)S(1)}, f32[1,64,256]{2,1,0:T(8,128)S(1)}, u32[]{:S(2)}, u32[]{:S(2)}) collective-permute-start(f32[1,64,256]{2,1,0:T(8,128)S(1)} %get-tuple-element.54), channel_id=1, source_target_pairs={{0,4},{4,8},{8,12},{12,16},{16,20},{20,24},{24,28},{1,5},{5,9},{9,... | collective-permute-start | bytes 196616 | tf_op jit(solution)/shard_map/ppermute | solution.py:20
  345.1 16.3 %collective-permute-start.44 = (f32[1,128,512]{1,2,0:T(8,128)}, f32[1,128,512]{1,2,0:T(8,128)S(1)}, u32[]{:S(2)}, u32[]{:S(2)}) collective-permute-start(f32[1,128,512]{1,2,0:T(8,128)} %bitcast.14), channel_id=1, source_target_pairs={{4,0},{8,4},{12,8},{16,12},{20,16},{24,20},{28,24},{5,1},{9,5},{13... | collective-permute-start | bytes 786440 | tf_op jit(solution)/shard_map/ppermute | solution.py:21
  349.8 11.6 %collective-permute-start.45 = (f32[1,128,512]{1,2,0:T(8,128)}, f32[1,128,512]{1,2,0:T(8,128)}, u32[]{:S(2)}, u32[]{:S(2)}) collective-permute-start(f32[1,128,512]{1,2,0:T(8,128)} %bitcast.16), channel_id=1, source_target_pairs={{0,4},{4,8},{8,12},{12,16},{16,20},{20,24},{24,28},{1,5},{5,9},{9,... | collective-permute-start | bytes 786440 | tf_op jit(solution)/shard_map/ppermute | solution.py:20
  368.0 15.5 %collective-permute-start.46 = (f32[6,1,512]{2,1,0:T(1,128)S(1)}, f32[6,1,512]{2,1,0:T(1,128)}, u32[]{:S(2)}, u32[]{:S(2)}) collective-permute-start(f32[6,1,512]{2,1,0:T(1,128)S(1)} %copy.153), channel_id=1, source_target_pairs={{1,0},{2,1},{3,2},{5,4},{6,5},{7,6},{9,8},{10,9},{11,10},{13,12},{... | collective-permute-start | bytes 36872 | tf_op jit(solution)/shard_map/ppermute | solution.py:21
  371.8 14.1 %collective-permute-start.47 = (f32[6,1,512]{2,1,0:T(1,128)}, f32[6,1,512]{2,1,0:T(1,128)}, u32[]{:S(2)}, u32[]{:S(2)}) collective-permute-start(f32[6,1,512]{2,1,0:T(1,128)} %copy.155), channel_id=1, source_target_pairs={{0,1},{1,2},{2,3},{4,5},{5,6},{6,7},{8,9},{9,10},{10,11},{12,13},{... | collective-permute-start | bytes 36872 | tf_op jit(solution)/shard_map/ppermute | solution.py:20
  407.2 8.0 %collective-permute-start.50 = (f32[6,1,512]{2,1,0:T(1,128)S(1)}, f32[6,1,512]{2,1,0:T(1,128)S(1)}, u32[]{:S(2)}, u32[]{:S(2)}) collective-permute-start(f32[6,1,512]{2,1,0:T(1,128)S(1)} %copy.159), channel_id=1, source_target_pairs={{1,0},{2,1},{3,2},{5,4},{6,5},{7,6},{9,8},{10,9},{11,10},{13,12},{... | collective-permute-start | bytes 36872 | tf_op jit(solution)/shard_map/ppermute | solution.py:21
  410.4 6.5 %collective-permute-start.51 = (f32[6,1,512]{2,1,0:T(1,128)S(1)}, f32[6,1,512]{2,1,0:T(1,128)S(1)}, u32[]{:S(2)}, u32[]{:S(2)}) collective-permute-start(f32[6,1,512]{2,1,0:T(1,128)S(1)} %copy.161), channel_id=1, source_target_pairs={{0,1},{1,2},{2,3},{4,5},{5,6},{6,7},{8,9},{9,10},{10,11},{12,13},{... | collective-permute-start | bytes 36872 | tf_op jit(solution)/shard_map/ppermute | solution.py:20
  423.8 8.6 %collective-permute-start.52 = (f32[1,128,512]{1,2,0:T(8,128)S(1)}, f32[1,128,512]{1,2,0:T(8,128)S(1)}, u32[]{:S(2)}, u32[]{:S(2)}) collective-permute-start(f32[1,128,512]{1,2,0:T(8,128)S(1)} %get-tuple-element.31), channel_id=1, source_target_pairs={{4,0},{8,4},{12,8},{16,12},{20,16},{24,20},{28,24},{5,1},{9,5},{13... | collective-permute-start | bytes 786440 | tf_op jit(solution)/shard_map/ppermute | solution.py:21
  425.1 8.4 %collective-permute-start.53 = (f32[1,128,512]{1,2,0:T(8,128)S(1)}, f32[1,128,512]{1,2,0:T(8,128)S(1)}, u32[]{:S(2)}, u32[]{:S(2)}) collective-permute-start(f32[1,128,512]{1,2,0:T(8,128)S(1)} %get-tuple-element.30), channel_id=1, source_target_pairs={{0,4},{4,8},{8,12},{12,16},{16,20},{20,24},{24,28},{1,5},{5,9},{9,... | collective-permute-start | bytes 786440 | tf_op jit(solution)/shard_map/ppermute | solution.py:20
  438.3 8.0 %collective-permute-start.54 = (f32[6,1,512]{2,1,0:T(1,128)S(1)}, f32[6,1,512]{2,1,0:T(1,128)S(1)}, u32[]{:S(2)}, u32[]{:S(2)}) collective-permute-start(f32[6,1,512]{2,1,0:T(1,128)S(1)} %copy.165), channel_id=1, source_target_pairs={{1,0},{2,1},{3,2},{5,4},{6,5},{7,6},{9,8},{10,9},{11,10},{13,12},{... | collective-permute-start | bytes 36872 | tf_op jit(solution)/shard_map/ppermute | solution.py:21
  441.5 6.5 %collective-permute-start.55 = (f32[6,1,512]{2,1,0:T(1,128)S(1)}, f32[6,1,512]{2,1,0:T(1,128)S(1)}, u32[]{:S(2)}, u32[]{:S(2)}) collective-permute-start(f32[6,1,512]{2,1,0:T(1,128)S(1)} %copy.167), channel_id=1, source_target_pairs={{0,1},{1,2},{2,3},{4,5},{5,6},{6,7},{8,9},{9,10},{10,11},{12,13},{... | collective-permute-start | bytes 36872 | tf_op jit(solution)/shard_map/ppermute | solution.py:20
  457.7 116.9 %all-gather.2.cloned.1.call-start = ((), (), s32[]{:S(2)}) async-start(), calls=%async_computation.1 | async-start | bytes 2621440 | tf_op jit(solution)/shard_map/all_gather | solution.py:121
  (63 other events, 547.3 us)
Sparse Core Ops, SparseCore 0:
  457.8 69.4 all-reduce.15
  529.0 45.5 all-gather.1
where the time goes:
time: 626 us; the launch traced here: 615 us
  starting transfers between devices  186 us (30%)
  local copies, waits for them, and re-layouts  181 us (29%)
  waiting for transfers between devices  135 us (22%)
  other arithmetic  97.5 us (16%)
  between operations  15.8 us (3%)
    ppermute x28, starting transfers between devices, with_halo(): before = lax.ppermute(last, axis, up)  149 us
    psum x1, waiting for transfers between devices, shards(): summed_faces = lax.psum(jnp.stack([low_part, high_part]), 'slab')  69.6 us
    reshape x1, local copies, waits for them, and re-layouts, children_sum(): blocks = field.reshape(x_cells // 2, 2, y_cells // 2, 2, z_cells // 2, 2)  69.2 us
    all_gather x1, waiting for transfers between devices, shards(): all_faces = lax.all_gather(summed_faces, 'pencil', axis=1, tiled=True)  44.4 us
    ppermute x28, starting transfers between devices, with_halo(): after = lax.ppermute(initial, axis, down)  36.1 us
    scatter-add x1, other arithmetic, add_rows(): jax.ops.segment_sum(rows_data, segment_ids, num_segments=slot_count + 1)  28.7 us
    slice x25, local copies, waits for them, and re-layouts, with_halo(): last = lax.slice_in_dim(x, length - width, length, axis=dim)  27.3 us
    concatenate x28, other arithmetic, with_halo(): x = jnp.concatenate([before, x, after], axis=dim)  26.3 us
  transfers between devices with their start and end apart: 58, of which 22 were waited for; matrix products, arithmetic and copies ran while one was open for 8% of the time, Pallas kernels for 0%

commit v1 on v0

v1 whole, which is shorter than its diff:
```python
import functools
import jax
import jax.numpy as jnp
from jax import lax
from jax.experimental import pallas as pl
from jax.experimental.pallas import tpu as pltpu
from jax.sharding import PartitionSpec as P

TILE = 128
W = 2.0 / 3.0
EDGE = 8
ROUNDS = 14
MESH = pl.DeviceIdType.MESH


def coefficient(level):
    return W * 4.0**level / 6.0


def split3(x):
    hi = x.astype(jnp.bfloat16)
    rest = x - hi.astype(jnp.float32)
    mid = rest.astype(jnp.bfloat16)
    lo = (rest - mid.astype(jnp.float32)).astype(jnp.bfloat16)
    return hi, mid, lo


def times01(x, table):
    hi, mid, lo = split3(x)
    dot = functools.partial(jnp.dot, preferred_element_type=jnp.float32)
    return dot(hi, table) + (dot(mid, table) + dot(lo, table))


def from01(table, x):
    hi, mid, lo = split3(x)
    dot = functools.partial(jnp.dot, preferred_element_type=jnp.float32)
    return dot(table, hi) + (dot(table, mid) + dot(table, lo))


def pair_table(fine, coarse, shift, transposed):
    shape = (fine, coarse) if not transposed else (coarse, fine)
    f = lax.broadcasted_iota(jnp.int32, shape, 1 if transposed else 0)
    c = lax.broadcasted_iota(jnp.int32, shape, 0 if transposed else 1)
    return (((f + shift) // 2) == c).astype(jnp.float32).astype(jnp.bfloat16)


def cycle_kernel(
    S, Q, cot, rhs,
    f0, f1, f2, g3, m0, m1, m2, m3, c0, c1, gc, bm, n0, n1, gm, bf, h0, h1,
    load_sem, send_sem, recv_sem,
):
    s, q = lax.axis_index("slab"), lax.axis_index("pencil")
    has = (s > 0, s < S - 1, q > 0, q < Q - 1)
    peers = (
        (lax.max(s - 1, 0), q), (lax.min(s + 1, S - 1), q),
        (s, lax.max(q - 1, 0)), (s, lax.min(q + 1, Q - 1)),
    )
    NX, NYL, NZL = cot.shape

    load = pltpu.make_async_copy(cot, f0.at[pl.ds(1, NX), pl.ds(EDGE, NYL)], load_sem)
    load.start()

    barrier = pltpu.get_barrier_semaphore()
    for d in range(4):
        @pl.when(has[d])
        def _():
            pl.semaphore_signal(barrier, inc=1, device_id=peers[d], device_id_type=MESH)
    pl.semaphore_wait(barrier, sum(h.astype(jnp.int32) for h in has))

    def sizes(buf):
        return buf.shape[0] - 2, buf.shape[1] - 2 * EDGE, buf.shape[2]

    def regions(buf):
        nx, ny, _ = sizes(buf)
        own_x, own_y = pl.ds(1, nx), pl.ds(EDGE, ny)
        src = (
            buf.at[1, own_y], buf.at[nx, own_y],
            buf.at[own_x, pl.ds(EDGE, EDGE)], buf.at[own_x, pl.ds(ny, EDGE)],
        )
        halo = (
            buf.at[0, own_y], buf.at[nx + 1, own_y],
            buf.at[own_x, pl.ds(0, EDGE)], buf.at[own_x, pl.ds(EDGE + ny, EDGE)],
        )
        return src, halo

    def copy(rnd, buf, d):
        src, halo = regions(buf)
        return pltpu.make_async_remote_copy(
            src_ref=src[d], dst_ref=halo[d ^ 1],
            send_sem=send_sem.at[rnd, d], recv_sem=recv_sem.at[rnd, d ^ 1],
            device_id=peers[d], device_id_type=MESH,
        )

    def start(rnd, buf, d):
        @pl.when(has[d])
        def _():
            copy(rnd, buf, d).start()

    def arrive(rnd, buf, d):
        src, halo = regions(buf)

        @pl.when(has[d])
        def _():
            pltpu.make_async_remote_copy(
                src_ref=src[d ^ 1], dst_ref=halo[d],
                send_sem=send_sem.at[rnd, d], recv_sem=recv_sem.at[rnd, d],
                device_id=peers[d], device_id_type=MESH,
            ).wait_recv()

    sent = []

    def clear(buf):
        _, halo = regions(buf)
        for d in range(4):
            @pl.when(jnp.logical_not(has[d]))
            def _():
                halo[d][...] = jnp.zeros(halo[d].shape, jnp.float32)

    def neighbours(buf, x, r0, rows):
        z = buf.shape[2]
        big = buf[x, pl.ds(r0, rows + 2 * EDGE), :]
        v = big[EDGE:EDGE + rows]
        nb = buf[x - 1, pl.ds(r0 + EDGE, rows), :] + buf[x + 1, pl.ds(r0 + EDGE, rows), :]
        nb = nb + pltpu.roll(big, 1, 0)[EDGE:EDGE + rows]
        nb = nb + pltpu.roll(big, rows + 2 * EDGE - 1, 0)[EDGE:EDGE + rows]
        lane = lax.broadcasted_iota(jnp.int32, (rows, z), 1)
        nb = nb + jnp.where(lane == 0, 0.0, pltpu.roll(v, 1, 1))
        nb = nb + jnp.where(lane == z - 1, 0.0, pltpu.roll(v, z - 1, 1))
        return v, nb

    def rows_of(buf):
        return min(32, sizes(buf)[1])

    def plane_op(buf, x_first, x_count, body):
        ny, rows = sizes(buf)[1], rows_of(buf)
        per = ny // rows

        def step(i, _):
            x = x_first + i // per
            r0 = pl.multiple_of((i % per) * rows, rows)
            body(x, r0, rows)
            return 0
        lax.fori_loop(0, x_count * per, step, 0)

    def sweep(rnd, buf, finish, out=None, between=None):
        nx = sizes(buf)[0]

        def body(x, r0, rows):
            v, nb = neighbours(buf, x, r0, rows)
            finish(x, r0, rows, v, nb)
        if out is not None:
            clear(out)
        if between is not None:
            between()
        arrive(rnd, buf, 2)
        arrive(rnd, buf, 3)
        if nx > 2:
            plane_op(buf, 2, nx - 2, body)
        arrive(rnd, buf, 0)
        if nx == 1:
            arrive(rnd, buf, 1)
        plane_op(buf, 1, 1, body)
        if out is not None:
            start(rnd + 1, out, 0)
            if nx == 1:
                start(rnd + 1, out, 1)
        if nx > 1:
            arrive(rnd, buf, 1)
            plane_op(buf, nx, 1, body)
            if out is not None:
                start(rnd + 1, out, 1)
        if out is not None:
            start(rnd + 1, out, 2)
            start(rnd + 1, out, 3)
            sent.append((rnd + 1, out))

    def put(out, x, r0, rows, value):
        out[x, pl.ds(r0 + EDGE, rows), :] = value

    def own(buf, x, r0, rows):
        return buf[x, pl.ds(r0 + EDGE, rows), :]

    def smooth_to(out, padded=True):
        def finish(x, r0, rows, v, nb):
            value = (1.0 - W) * v + (W / 6.0) * nb
            if padded:
                put(out, x, r0, rows, value)
            else:
                out[x - 1, pl.ds(r0, rows), :] = value
        return finish

    def restrict(src, dst):
        x, y, z = src.shape
        sz = pair_table(z, z // 2, 0, False)
        sy = pair_table(y, y // 2, 0, True)
        for j in range(x // 2):
            both = src[2 * j] + src[2 * j + 1]
            half = times01(both, sz)
            dst[1 + j, pl.ds(EDGE, y // 2), :] = from01(sy, half)

    def prolong(src, dst):
        nx, ny, z = sizes(src)
        pz = pair_table(2 * z, z, 0, True)
        py = pair_table(2 * ny + 2 * EDGE, ny + 2 * EDGE, EDGE, False)
        pc = pair_table(2 * ny, ny, 0, False)
        for j in range(nx + 2):
            if j == 0 or j == nx + 1:
                wide = times01(src[j, pl.ds(EDGE, ny), :], pz)
                dst[0 if j == 0 else 2 * nx + 1, pl.ds(EDGE, 2 * ny), :] = 0.125 * from01(pc, wide)
            else:
                wide = times01(src[j], pz)
                value = 0.125 * from01(py, wide)
                dst[2 * j - 1] = value
                dst[2 * j] = value

    def send_all(rnd, buf):
        for d in range(4):
            start(rnd, buf, d)
        sent.append((rnd, buf))

    def arrive_all(rnd, buf):
        for d in range(4):
            arrive(rnd, buf, d)

    clear(f0)
    load.wait()
    send_all(0, f0)
    sweep(0, f0, smooth_to(f1), f1)
    sweep(1, f1, smooth_to(f2), f2)
    sweep(2, f2, smooth_to(g3, False))
    clear(m0)
    restrict(g3, m0)
    send_all(3, m0)
    sweep(3, m0, smooth_to(m1), m1)
    sweep(4, m1, smooth_to(m2), m2)
    sweep(5, m2, smooth_to(m3, False))
    clear(c0)
    restrict(m3, c0)
    send_all(6, c0)
    sweep(6, c0, smooth_to(c1), c1)

    def coarse_total(x, r0, rows, v, nb):
        value = (1.0 - W) * v + (W / 6.0) * nb
        put(gc, x, r0, rows, coefficient(2) * (own(c0, x, r0, rows) + own(c1, x, r0, rows) + value))
    sweep(7, c1, coarse_total, gc)
    arrive_all(8, gc)
    prolong(gc, bm)

    def medium_correct(x, r0, rows):
        v, nb = neighbours(bm, x, r0, rows)
        put(n0, x, r0, rows, m3[x - 1, pl.ds(r0, rows), :] - (6.0 * v - nb) * 0.25)
    clear(n0)
    plane_op(n0, 1, sizes(n0)[0], medium_correct)
    send_all(9, n0)
    sweep(9, n0, smooth_to(n1), n1)

    def medium_total(x, r0, rows, v, nb):
        value = (1.0 - W) * v + (W / 6.0) * nb
        total = own(m0, x, r0, rows) + own(m1, x, r0, rows) + own(m2, x, r0, rows)
        total = total + own(n0, x, r0, rows) + v + value
        put(gm, x, r0, rows, coefficient(1) * total + own(bm, x, r0, rows))
    sweep(10, n1, medium_total, gm)
    arrive_all(11, gm)
    prolong(gm, bf)

    def fine_correct(x, r0, rows):
        v, nb = neighbours(bf, x, r0, rows)
        put(h0, x, r0, rows, g3[x - 1, pl.ds(r0, rows), :] - (6.0 * v - nb))
    clear(h0)
    nx = sizes(h0)[0]
    plane_op(h0, 1, 1, fine_correct)
    start(12, h0, 0)
    plane_op(h0, nx, 1, fine_correct)
    start(12, h0, 1)
    plane_op(h0, 2, nx - 2, fine_correct)
    start(12, h0, 2)
    start(12, h0, 3)
    sent.append((12, h0))

    def gather_first():
        def body(x, r0, rows):
            total = own(f0, x, r0, rows) + own(f1, x, r0, rows) + own(f2, x, r0, rows)
            total = total + own(h0, x, r0, rows)
            rhs[x - 1, pl.ds(r0, rows), :] = coefficient(0) * total + own(bf, x, r0, rows)
        plane_op(h0, 1, nx, body)
    sweep(12, h0, smooth_to(h1), h1, between=gather_first)

    def fine_total(x, r0, rows, v, nb):
        value = (1.0 - W) * v + (W / 6.0) * nb
        before = rhs[x - 1, pl.ds(r0, rows), :]
        rhs[x - 1, pl.ds(r0, rows), :] = before + coefficient(0) * (v + value)
    sweep(13, h1, fine_total)
    for rnd, buf in sent:
        for d in range(4):
            @pl.when(has[d])
            def _():
                copy(rnd, buf, d).wait_send()


def run_cycle(cotangent):
    S, Q = lax.axis_size("slab"), lax.axis_size("pencil")
    x, y, z = cotangent.shape

    def padded(level):
        k = 2**level
        return pltpu.VMEM((x // k + 2, y // k + 2 * EDGE, z // k), jnp.float32)

    def plain(level):
        k = 2**level
        return pltpu.VMEM((x // k, y // k, z // k), jnp.float32)
    scratch = [padded(0)] * 3 + [plain(0)] + [padded(1)] * 3 + [plain(1)]
    scratch += [padded(2)] * 3 + [padded(1)] * 4 + [padded(0)] * 3
    scratch += [
        pltpu.SemaphoreType.DMA,
        pltpu.SemaphoreType.DMA((ROUNDS, 4)),
        pltpu.SemaphoreType.DMA((ROUNDS, 4)),
    ]
    return pl.pallas_call(
        functools.partial(cycle_kernel, S, Q),
        out_shape=jax.ShapeDtypeStruct(cotangent.shape, jnp.float32),
        in_specs=[pl.BlockSpec(memory_space=pl.ANY)],
        out_specs=pl.BlockSpec(memory_space=pltpu.VMEM),
        scratch_shapes=scratch,
        compiler_params=pltpu.CompilerParams(
            collective_id=0, has_side_effects=True, vmem_limit_bytes=48 * 2**20
        ),
        name="vcycle",
    )(cotangent)


def source_rows(seg_rows, owners, offsets, tile_size):
    starts = jnp.cumsum(seg_rows, axis=1) - seg_rows
    position = jnp.arange(tile_size, dtype=jnp.int32)[None, None, :]
    inside = (position >= starts[:, :, None]) & (position < (starts + seg_rows)[:, :, None])
    value = owners[:, :, None] * tile_size + offsets[:, :, None] + position - starts[:, :, None]
    return jnp.sum(jnp.where(inside, value, 0), axis=1)


def tile_rows(faces, tile_size):
    face_count, y_cells, z_cells = faces.shape
    blocks = faces.reshape(
        face_count, y_cells // tile_size, tile_size, z_cells // tile_size, tile_size
    )
    return blocks.transpose(0, 1, 3, 2, 4).reshape(-1, tile_size)


def shards(cotangent, seg_rows, owners, offsets):
    rhs_grad = run_cycle(cotangent)
    x_cells = rhs_grad.shape[0]
    slab_index, slab_count = lax.axis_index("slab"), lax.axis_size("slab")
    low_part = jnp.where(slab_index == 0, rhs_grad[0], 0.0)
    high_part = jnp.where(slab_index == slab_count - 1, rhs_grad[x_cells - 1], 0.0)
    summed_faces = lax.psum(jnp.stack([low_part, high_part]), "slab")
    all_faces = lax.all_gather(summed_faces, "pencil", axis=1, tiled=True)
    all_rows = tile_rows(all_faces, TILE)
    targets = source_rows(seg_rows, owners, offsets, TILE).reshape(-1)
    first_row = lax.axis_index(("slab", "pencil")) * TILE
    hot = (targets[None, :] - first_row) == jnp.arange(TILE, dtype=jnp.int32)[:, None]
    owned = jnp.dot(hot.astype(jnp.float32), all_rows, precision=lax.Precision.HIGHEST)
    return (rhs_grad, owned.reshape(1, TILE, TILE))


def solution(mesh):
    return jax.shard_map(
        shards,
        mesh=mesh,
        in_specs=(P("slab", "pencil", None), P(), P(), P()),
        out_specs=(P("slab", "pencil", None), P(("slab", "pencil"), None, None)),
        check_vma=False,
    )
```

time: 626 us -> 197 us (0.31); the launches traced: 615 us -> 197 us
  starting transfers between devices: 186 us -> 0.08 us
  local copies, waits for them, and re-layouts: 181 us -> 4.41 us
  other arithmetic: 97.5 us -> 1.05 us
  Pallas kernels: 0 us -> 67.9 us
  waiting for transfers between devices: 135 us -> 107 us
    ppermute x56 -> x0, starting transfers between devices: 186 us -> none  [the longest x28 149 us: with_halo(): before = lax.ppermute(last, axis, up)]
    reshape x2 -> x0, local copies, waits for them, and re-layouts: 69.8 us -> none  [the longest x1 69.2 us: children_sum(): blocks = field.reshape(x_cells // 2, 2, y_cells // 2, 2, z_cells // 2, 2)]
    pallas_call x0 -> x1, Pallas kernels: none -> 67.9 us  [run_cycle(): pl.pallas_call(functools.partial(cycle_kernel, S, Q), out_shape=jax.Shape...]
    slice x33 -> x0, local copies, waits for them, and re-layouts: 38.8 us -> none  [the longest x25 27.3 us: with_halo(): last = lax.slice_in_dim(x, length - width, length, axis=dim)]
    scatter-add x1 -> x0, other arithmetic: 28.7 us -> none  [add_rows(): jax.ops.segment_sum(rows_data, segment_ids, num_segments=slot_count + 1)]
    concatenate x28 -> x0, other arithmetic: 26.3 us -> none  [with_halo(): x = jnp.concatenate([before, x, after], axis=dim)]
    reduce_sum x3 -> x0, other arithmetic: 25 us -> none  [children_sum(): return jnp.sum(blocks, axis=(1, 3, 5))]
    ppermute x14 -> x0, local copies, waits for them, and re-layouts: 23.4 us -> none  [the longest x7 12.3 us: with_halo(): before = lax.ppermute(last, axis, up)]
  transfers between devices with their start and end apart: 58 -> 2, of which waited for: 22 -> 2; matrix products, arithmetic and copies ran while one was open for 8% -> 0% of each run, Pallas kernels for 0% -> 0%
where the time goes in v1:
time: 197 us
  waiting for transfers between devices  107 us (54%)
  Pallas kernels  67.9 us (34%)
  between operations  14.1 us (7%)
  local copies, waits for them, and re-layouts  4.41 us (2%)
  matrix products  2.11 us (1%)
    pallas_call x1, Pallas kernels, run_cycle(): pl.pallas_call(functools.partial(cycle_kernel, S, Q), out_shape=jax.Shape...  67.9 us
    psum x1, waiting for transfers between devices, shards(): summed_faces = lax.psum(jnp.stack([low_part, high_part]), 'slab')  60.3 us
    all_gather x1, waiting for transfers between devices, shards(): all_faces = lax.all_gather(summed_faces, 'pencil', axis=1, tiled=True)  46.7 us
  transfers between devices with their start and end apart: 2, of which 2 were waited for; matrix products, arithmetic and copies ran while one was open for 0% of the time, Pallas kernels for 0%

profile of v1, /device:TPU:0, one launch (start us, length us, event | category | flops | bytes accessed | tf_op | source)
XLA Modules:
  0.0 196.7 jit_solution(3442824815883933914)
XLA Ops:
  7.2 0.0 all-reduce.2.cloned.1.call-start
  7.2 0.0 copy-start
  7.2 1.2 copy-done
  8.4 67.9 %vcycle.1 = f32[4,128,512]{2,1,0:T(8,128)S(1)} custom-call(f32[4,128,512]{2,1,0:T(8,128)S(1)} %copy-done), custom_call_target="tpu_custom_call" | custom-call | tf_op jit(solution)/shard_map/vcycle/pallas_call | solution.py:318
  76.4 0.0 copy-start.1
  76.4 0.0 copy-start.2
  76.4 0.0 copy-start.3
  76.5 0.8 pad_maximum_fusion
  77.3 0.0 all-reduce.2.cloned.1.call-update
  77.3 0.0 all-gather.2.cloned.1.call-start
  77.4 60.3 %all-reduce.2.cloned.1.call-done = f32[2,128,512]{2,1,0:T(8,128)} async-done(((f32[2,128,512]{2,1,0:T(8,128)}), f32[2,128,512]{2,1,0:T(8,128)}) %all-reduce.2.cloned.1.call-update) | async-done | bytes 524304 | tf_op jit(solution)/shard_map/psum | solution.py:353
  137.7 0.0 all-gather.2.cloned.1.call-update
  137.7 0.0 copy-done.1
  137.7 0.0 copy-done.2
  137.7 0.0 copy-done.3
  137.8 0.1 select_reduce_fusion
  137.9 46.7 %all-gather.2.cloned.1.call-done = f32[2,512,512]{2,1,0:T(8,128)} async-done(((f32[2,128,512]{2,1,0:T(8,128)}), f32[2,512,512]{2,1,0:T(8,128)}) %all-gather.2.cloned.1.call-update) | async-done | bytes 2097168 | tf_op jit(solution)/shard_map/all_gather | solution.py:354
  184.6 1.9 reshape.27
  186.5 0.3 copy.13
  186.8 2.1 %fusion.1 = f32[1,128,128]{2,1,0:T(8,128)} fusion(f32[4096,128]{1,0:T(8,128)S(1)} %bitcast.8, s32[4096]{0:T(1024)S(1)} %subtract_bitcast_fusion), kind=kOutput, calls=%fused_computation.2 | convolution fusion | flops 805830656 | bytes 2179072 | tf_op jit(solution)/shard_map/dot_general | solution.py:359
  188.9 1.0 copy.16
  (5 shorter events, 0.1 us)
Async XLA Ops:
  7.2 130.5 %all-reduce.2.cloned.1.call-start = ((), (), s32[]{:S(2)}) async-start(), calls=%async_computation | async-start | bytes 1048576 | tf_op jit(solution)/shard_map/psum | solution.py:353
  7.2 1.2 copy-start
  76.4 61.3 %copy-start.1 = (s32[32,4]{0,1:T(4,128)S(1)}, s32[32,4]{0,1:T(4,128)}, u32[]{:S(2)}) copy-start(s32[32,4]{0,1:T(4,128)} %param.5) | copy-start | bytes 1540
  76.4 61.3 %copy-start.2 = (s32[32,4]{0,1:T(4,128)S(1)}, s32[32,4]{0,1:T(4,128)}, u32[]{:S(2)}) copy-start(s32[32,4]{0,1:T(4,128)} %param.7) | copy-start | bytes 1540
  76.4 61.3 %copy-start.3 = (s32[32,4]{0,1:T(4,128)S(1)}, s32[32,4]{0,1:T(4,128)}, u32[]{:S(2)}) copy-start(s32[32,4]{0,1:T(4,128)} %param.6) | copy-start | bytes 1540
  77.3 107.3 %all-gather.2.cloned.1.call-start = ((), (), s32[]{:S(2)}) async-start(), calls=%async_computation.1 | async-start | bytes 2621440 | tf_op jit(solution)/shard_map/all_gather | solution.py:354
Sparse Core Ops, SparseCore 0:
  77.4 60.1 all-reduce.1
  139.3 45.2 all-gather.1

commit v2 on v1

--- a/solution.py
+++ b/solution.py
@@ -10,6 +10,7 @@
 W = 2.0 / 3.0
 EDGE = 8
 ROUNDS = 14
+CHUNKS = 4
 MESH = pl.DeviceIdType.MESH
 
 
@@ -44,10 +45,122 @@
     return (((f + shift) // 2) == c).astype(jnp.float32).astype(jnp.bfloat16)
 
 
+def face_return(
+    s, q, S, Q, pieces, goal, rhs, parent, fa, rows_buf, part_out, part_in,
+    piece_send, piece_recv, ring_send, ring_recv, part_send, part_recv,
+):
+    NX, NYL, NZL = rhs.shape
+    R = NYL // pieces
+    tiles_z = NZL // TILE
+    holders = ((0, 0, 0), (1, S - 1, NX - 1))
+
+    def piece(face, plane, k):
+        return pltpu.make_async_remote_copy(
+            src_ref=rhs.at[plane, pl.ds(k * R, R)], dst_ref=fa.at[face, q],
+            send_sem=piece_send.at[face, k], recv_sem=piece_recv.at[face],
+            device_id=(k, q), device_id_type=MESH,
+        )
+    for face, slab, plane in holders:
+        @pl.when(s == slab)
+        def _():
+            for k in range(pieces):
+                if k != slab:
+                    piece(face, plane, k).start()
+            if slab < pieces:
+                fa[face, q] = rhs[plane, pl.ds(slab * R, R), :]
+
+    def ring(k):
+        return pltpu.make_async_remote_copy(
+            src_ref=fa.at[:, q], dst_ref=fa.at[:, q],
+            send_sem=ring_send.at[k], recv_sem=ring_recv.at[k],
+            device_id=(s, lax.rem(q + k, Q)), device_id_type=MESH,
+        )
+
+    def ring_arrival(k):
+        source = lax.rem(q + Q - k, Q)
+        return pltpu.make_async_remote_copy(
+            src_ref=fa.at[:, source], dst_ref=fa.at[:, source],
+            send_sem=ring_send.at[k], recv_sem=ring_recv.at[k],
+            device_id=(s, source), device_id_type=MESH,
+        )
+
+    def part(k):
+        return pltpu.make_async_remote_copy(
+            src_ref=part_out.at[k], dst_ref=part_in.at[k],
+            send_sem=part_send.at[k], recv_sem=part_recv.at[k],
+            device_id=(lax.rem(s + k, S), q), device_id_type=MESH,
+        )
+
+    @pl.when(s < pieces)
+    def _():
+        for face, slab, plane in holders:
+            @pl.when(s != slab)
+            def _():
+                pltpu.make_async_remote_copy(
+                    src_ref=fa.at[face, q], dst_ref=fa.at[face, q],
+                    send_sem=piece_send.at[face, 0], recv_sem=piece_recv.at[face],
+                    device_id=(slab, q), device_id_type=MESH,
+                ).wait_recv()
+        for k in range(1, Q):
+            ring(k).start()
+        for k in range(1, Q):
+            ring_arrival(k).wait_recv()
+        for face in range(2):
+            for a in range(Q):
+                for b in range(tiles_z):
+                    t = (face * Q + a) * tiles_z + b
+                    rows_buf[pl.ds(t * R, R), :] = fa[face, a, :, pl.ds(b * TILE, TILE)]
+        hi, mid, lo = split3(rows_buf[...])
+        dot = functools.partial(jnp.dot, preferred_element_type=jnp.float32)
+        count = rows_buf.shape[0]
+        local = lax.broadcasted_iota(jnp.int32, (TILE, count), 0)
+        for k in list(range(1, S)) + [0]:
+            owner = lax.rem(s + k, S) * Q + q
+            shifted = goal[...] - owner * TILE
+            hot = (shifted == local).astype(jnp.float32).astype(jnp.bfloat16)
+            part_out[k] = dot(hot, hi) + (dot(hot, mid) + dot(hot, lo))
+            if k > 0:
+                part(k).start()
+
+    total = None
+    if pieces == S:
+        total = part_out[0]
+        for k in range(1, S):
+            part(k).wait_recv()
+            total = total + part_in[k]
+        parent[0] = total
+    else:
+        parent[...] = jnp.zeros_like(parent)
+
+        @pl.when(s < pieces)
+        def _():
+            parent[0] = part_out[0]
+        for k in range(1, S):
+            @pl.when(lax.rem(s + S - k, S) < pieces)
+            def _():
+                part(k).wait_recv()
+                parent[0] += part_in[k]
+
+    for face, slab, plane in holders:
+        @pl.when(s == slab)
+        def _():
+            for k in range(pieces):
+                if k != slab:
+                    piece(face, plane, k).wait_send()
+
+    @pl.when(s < pieces)
+    def _():
+        for k in range(1, Q):
+            ring(k).wait_send()
+        for k in range(1, S):
+            part(k).wait_send()
+
+
 def cycle_kernel(
-    S, Q, cot, rhs,
+    S, Q, pieces, cot, goal, rhs, parent,
     f0, f1, f2, g3, m0, m1, m2, m3, c0, c1, gc, bm, n0, n1, gm, bf, h0, h1,
-    load_sem, send_sem, recv_sem,
+    fa, rows_buf, part_out, part_in,
+    load_sem, send_sem, recv_sem, piece_send, piece_recv, ring_send, ring_recv, part_send, part_recv,
 ):
     s, q = lax.axis_index("slab"), lax.axis_index("pencil")
     has = (s > 0, s < S - 1, q > 0, q < Q - 1)
@@ -61,18 +174,24 @@
     load.start()
 
     barrier = pltpu.get_barrier_semaphore()
-    for d in range(4):
-        @pl.when(has[d])
-        def _():
-            pl.semaphore_signal(barrier, inc=1, device_id=peers[d], device_id_type=MESH)
-    pl.semaphore_wait(barrier, sum(h.astype(jnp.int32) for h in has))
+    for k in range(1, S):
+        pl.semaphore_signal(
+            barrier, inc=1, device_id=(lax.rem(s + k, S), q), device_id_type=MESH)
+    for k in range(1, Q):
+        pl.semaphore_signal(
+            barrier, inc=1, device_id=(s, lax.rem(q + k, Q)), device_id_type=MESH)
+    pl.semaphore_wait(barrier, S + Q - 2)
 
     def sizes(buf):
         return buf.shape[0] - 2, buf.shape[1] - 2 * EDGE, buf.shape[2]
 
-    def regions(buf):
+    def chunks(buf, d):
         nx, ny, _ = sizes(buf)
-        own_x, own_y = pl.ds(1, nx), pl.ds(EDGE, ny)
+        return CHUNKS if d < 2 and nx > 2 else 1
+
+    def regions(buf, c=0, n=1):
+        nx, ny, _ = sizes(buf)
+        own_x, own_y = pl.ds(1, nx), pl.ds(EDGE + c * (ny // n), ny // n)
         src = (
             buf.at[1, own_y], buf.at[nx, own_y],
             buf.at[own_x, pl.ds(EDGE, EDGE)], buf.at[own_x, pl.ds(ny, EDGE)],
@@ -83,29 +202,32 @@
         )
         return src, halo
 
-    def copy(rnd, buf, d):
-        src, halo = regions(buf)
+    def copy(rnd, buf, d, c):
+        src, halo = regions(buf, c, chunks(buf, d))
         return pltpu.make_async_remote_copy(
             src_ref=src[d], dst_ref=halo[d ^ 1],
-            send_sem=send_sem.at[rnd, d], recv_sem=recv_sem.at[rnd, d ^ 1],
+            send_sem=send_sem.at[rnd, d, c], recv_sem=recv_sem.at[rnd, d ^ 1, c],
             device_id=peers[d], device_id_type=MESH,
         )
 
-    def start(rnd, buf, d):
+    def start(rnd, buf, d, c=None):
         @pl.when(has[d])
         def _():
-            copy(rnd, buf, d).start()
-
-    def arrive(rnd, buf, d):
-        src, halo = regions(buf)
+            for i in range(chunks(buf, d)) if c is None else (c,):
+                copy(rnd, buf, d, i).start()
+
+    def arrive(rnd, buf, d, c=None):
+        n = chunks(buf, d)
 
         @pl.when(has[d])
         def _():
-            pltpu.make_async_remote_copy(
-                src_ref=src[d ^ 1], dst_ref=halo[d],
-                send_sem=send_sem.at[rnd, d], recv_sem=recv_sem.at[rnd, d],
-                device_id=peers[d], device_id_type=MESH,
-            ).wait_recv()
+            for i in range(n) if c is None else (c,):
+                src, halo = regions(buf, i, n)
+                pltpu.make_async_remote_copy(
+                    src_ref=src[d ^ 1], dst_ref=halo[d],
+                    send_sem=send_sem.at[rnd, d, i], recv_sem=recv_sem.at[rnd, d, i],
+                    device_id=peers[d], device_id_type=MESH,
+                ).wait_recv()
 
     sent = []
 
@@ -156,18 +278,25 @@
         arrive(rnd, buf, 3)
         if nx > 2:
             plane_op(buf, 2, nx - 2, body)
-        arrive(rnd, buf, 0)
-        if nx == 1:
+            rows = sizes(buf)[1] // CHUNKS
+            for c in range(CHUNKS):
+                for d, x in ((0, 1), (1, nx)):
+                    arrive(rnd, buf, d, c)
+                    body(x, c * rows, rows)
+                    if out is not None:
+                        start(rnd + 1, out, d, c)
+        elif nx == 2:
+            for d in range(2):
+                arrive(rnd, buf, d)
+                plane_op(buf, 1 + d, 1, body)
+                if out is not None:
+                    start(rnd + 1, out, d)
+        else:
+            arrive(rnd, buf, 0)
             arrive(rnd, buf, 1)
-        plane_op(buf, 1, 1, body)
-        if out is not None:
-            start(rnd + 1, out, 0)
-            if nx == 1:
-                start(rnd + 1, out, 1)
-        if nx > 1:
-            arrive(rnd, buf, 1)
-            plane_op(buf, nx, 1, body)
+            plane_op(buf, 1, 1, body)
             if out is not None:
+                start(rnd + 1, out, 0)
                 start(rnd + 1, out, 1)
         if out is not None:
             start(rnd + 1, out, 2)
@@ -290,16 +419,25 @@
         before = rhs[x - 1, pl.ds(r0, rows), :]
         rhs[x - 1, pl.ds(r0, rows), :] = before + coefficient(0) * (v + value)
     sweep(13, h1, fine_total)
+    face_return(
+        s, q, S, Q, pieces, goal, rhs, parent, fa, rows_buf, part_out, part_in,
+        piece_send, piece_recv, ring_send, ring_recv, part_send, part_recv)
     for rnd, buf in sent:
         for d in range(4):
             @pl.when(has[d])
             def _():
-                copy(rnd, buf, d).wait_send()
-
-
-def run_cycle(cotangent):
+                for c in range(chunks(buf, d)):
+                    copy(rnd, buf, d, c).wait_send()
+
+
+def run_cycle(cotangent, seg_rows, owners, offsets):
     S, Q = lax.axis_size("slab"), lax.axis_size("pencil")
     x, y, z = cotangent.shape
+    pieces = min(S, y // EDGE)
+    R = y // pieces
+    targets = source_rows(seg_rows, owners, offsets, TILE)
+    first = jnp.minimum(lax.axis_index("slab"), pieces - 1) * R
+    goal = lax.dynamic_slice_in_dim(targets, first, R, axis=1).reshape(1, -1)
 
     def padded(level):
         k = 2**level
@@ -311,21 +449,34 @@
     scratch = [padded(0)] * 3 + [plain(0)] + [padded(1)] * 3 + [plain(1)]
     scratch += [padded(2)] * 3 + [padded(1)] * 4 + [padded(0)] * 3
     scratch += [
+        pltpu.VMEM((2, Q, R, z), jnp.float32),
+        pltpu.VMEM((goal.shape[1], TILE), jnp.float32),
+        pltpu.VMEM((S, TILE, TILE), jnp.float32),
+        pltpu.VMEM((S, TILE, TILE), jnp.float32),
         pltpu.SemaphoreType.DMA,
-        pltpu.SemaphoreType.DMA((ROUNDS, 4)),
-        pltpu.SemaphoreType.DMA((ROUNDS, 4)),
+        pltpu.SemaphoreType.DMA((ROUNDS, 4, CHUNKS)),
+        pltpu.SemaphoreType.DMA((ROUNDS, 4, CHUNKS)),
+        pltpu.SemaphoreType.DMA((2, pieces)),
+        pltpu.SemaphoreType.DMA((2,)),
+        pltpu.SemaphoreType.DMA((Q,)),
+        pltpu.SemaphoreType.DMA((Q,)),
+        pltpu.SemaphoreType.DMA((S,)),
+        pltpu.SemaphoreType.DMA((S,)),
     ]
     return pl.pallas_call(
-        functools.partial(cycle_kernel, S, Q),
-        out_shape=jax.ShapeDtypeStruct(cotangent.shape, jnp.float32),
-        in_specs=[pl.BlockSpec(memory_space=pl.ANY)],
-        out_specs=pl.BlockSpec(memory_space=pltpu.VMEM),
+        functools.partial(cycle_kernel, S, Q, pieces),
+        out_shape=(
+            jax.ShapeDtypeStruct(cotangent.shape, jnp.float32),
+            jax.ShapeDtypeStruct((1, TILE, TILE), jnp.float32),
+        ),
+        in_specs=[pl.BlockSpec(memory_space=pl.ANY), pl.BlockSpec(memory_space=pltpu.VMEM)],
+        out_specs=(pl.BlockSpec(memory_space=pltpu.VMEM), pl.BlockSpec(memory_space=pltpu.VMEM)),
         scratch_shapes=scratch,
         compiler_params=pltpu.CompilerParams(
             collective_id=0, has_side_effects=True, vmem_limit_bytes=48 * 2**20
         ),
         name="vcycle",
-    )(cotangent)
+    )(cotangent, goal)
 
 
 def source_rows(seg_rows, owners, offsets, tile_size):
@@ -336,28 +487,9 @@
     return jnp.sum(jnp.where(inside, value, 0), axis=1)
 
 
-def tile_rows(faces, tile_size):
-    face_count, y_cells, z_cells = faces.shape
-    blocks = faces.reshape(
-        face_count, y_cells // tile_size, tile_size, z_cells // tile_size, tile_size
-    )
-    return blocks.transpose(0, 1, 3, 2, 4).reshape(-1, tile_size)
-
-
 def shards(cotangent, seg_rows, owners, offsets):
-    rhs_grad = run_cycle(cotangent)
-    x_cells = rhs_grad.shape[0]
-    slab_index, slab_count = lax.axis_index("slab"), lax.axis_size("slab")
-    low_part = jnp.where(slab_index == 0, rhs_grad[0], 0.0)
-    high_part = jnp.where(slab_index == slab_count - 1, rhs_grad[x_cells - 1], 0.0)
-    summed_faces = lax.psum(jnp.stack([low_part, high_part]), "slab")
-    all_faces = lax.all_gather(summed_faces, "pencil", axis=1, tiled=True)
-    all_rows = tile_rows(all_faces, TILE)
-    targets = source_rows(seg_rows, owners, offsets, TILE).reshape(-1)
-    first_row = lax.axis_index(("slab", "pencil")) * TILE
-    hot = (targets[None, :] - first_row) == jnp.arange(TILE, dtype=jnp.int32)[:, None]
-    owned = jnp.dot(hot.astype(jnp.float32), all_rows, precision=lax.Precision.HIGHEST)
-    return (rhs_grad, owned.reshape(1, TILE, TILE))
+    rhs_grad, parent_grad = run_cycle(cotangent, seg_rows, owners, offsets)
+    return (rhs_grad, parent_grad)
 
 
 def solution(mesh):

time: 197 us -> 92.6 us (0.47)
  waiting for transfers between devices: 107 us -> 0 us
  Pallas kernels: 67.9 us -> 86.7 us
  between operations: 14.1 us -> 0.67 us
  matrix products: 2.11 us -> 0 us
    psum x1 -> x0, waiting for transfers between devices: 60.3 us -> none  [shards(): summed_faces = lax.psum(jnp.stack([low_part, high_part]), 'slab')]
    all_gather x1 -> x0, waiting for transfers between devices: 46.7 us -> none  [shards(): all_faces = lax.all_gather(summed_faces, 'pencil', axis=1, tiled=True)]
    pallas_call x1, Pallas kernels: 67.9 us -> 86.7 us  [run_cycle(): pl.pallas_call(functools.partial(cycle_kernel, S, Q, pieces), out_shape=(...]
    reshape x2 -> x1, local copies, waits for them, and re-layouts: 2.21 us -> 0.08 us  [run_cycle(): goal = lax.dynamic_slice_in_dim(targets, first, R, axis=1).reshape(1, -1)]
    dot_general x1 -> x0, matrix products: 2.11 us -> none  [shards(): jnp.dot(hot.astype(jnp.float32), all_rows, precision=lax.Precision.HIGHEST)]
    unnamed x9 -> x10, local copies, waits for them, and re-layouts: 2.21 us -> 4.19 us
  transfers between devices with their start and end apart: 2 -> 0, of which waited for: 2 -> 0; matrix products, arithmetic and copies ran while one was open for 0% -> 0% of each run, Pallas kernels for 0% -> 0%
where the time goes in v2:
time: 92.6 us; the launch traced here: 91.9 us
  Pallas kernels  86.7 us (94%)
  local copies, waits for them, and re-layouts  4.35 us (5%)
    pallas_call x1, Pallas kernels, run_cycle(): pl.pallas_call(functools.partial(cycle_kernel, S, Q, pieces), out_shape=(...  86.7 us
    unnamed x10, local copies, waits for them, and re-layouts  4.19 us

profile of v2, /device:TPU:0, one launch (start us, length us, event | category | flops | bytes accessed | tf_op | source)
XLA Modules:
  0.0 91.9 jit_solution(9136181745999740694)
XLA Ops:
  0.6 0.0 copy-start.1
  0.6 0.7 copy-done.1
  1.4 0.0 copy-start.2
  1.4 0.0 copy-start.3
  1.4 0.7 copy-done.2
  2.0 0.0 copy-done.3
  2.1 0.1 select_reduce_fusion
  2.2 0.1 constant_dynamic-slice_fusion
  2.3 0.1 reshape.12.goal
  2.3 0.0 copy-start
  2.3 1.2 %copy-done = f32[4,128,512]{2,1,0:T(8,128)S(1)} copy-done((f32[4,128,512]{2,1,0:T(8,128)S(1)}, f32[4,128,512]{2,1,0:T(8,128)}, u32[]{:S(2)}) %copy-start) | copy-done | bytes 1048600
  3.6 86.7 %vcycle.1 = (f32[4,128,512]{2,1,0:T(8,128)S(1)}, f32[1,128,128]{2,1,0:T(8,128)S(1)}) custom-call(f32[4,128,512]{2,1,0:T(8,128)S(1)} %copy-done, s32[1,512]{1,0:T(1,128)S(1)} %reshape.12.goal), custom_call_target="tpu_custom_call" | custom-call | tf_op jit(solution)/shard_map/vcycle/pallas_call | solution.py:466
  90.3 1.0 %copy.14 = f32[4,128,512]{2,1,0:T(8,128)} copy(f32[4,128,512]{2,1,0:T(8,128)S(1)} %get-tuple-element.4) | data formatting | bytes 2097152
  91.3 0.6 copy.15
  (3 shorter events, 0.0 us)
Async XLA Ops:
  0.6 0.7 copy-start.1
  1.4 0.7 copy-start.2
  1.4 0.7 copy-start.3
  2.3 1.2 %copy-start = (f32[4,128,512]{2,1,0:T(8,128)S(1)}, f32[4,128,512]{2,1,0:T(8,128)}, u32[]{:S(2)}) copy-start(f32[4,128,512]{2,1,0:T(8,128)} %cot.1) | copy-start | bytes 3145732

commit v3 on v2

v3 whole, which is shorter than its diff:
```python
import functools
import jax
import jax.numpy as jnp
from jax import lax
from jax.experimental import pallas as pl
from jax.experimental.pallas import tpu as pltpu
from jax.sharding import PartitionSpec as P

TILE = 128
W = 2.0 / 3.0
EDGE = 8
ROUNDS = 14
CHUNKS = 4
MESH = pl.DeviceIdType.MESH


def coefficient(level):
    return W * 4.0**level / 6.0


def split3(x):
    hi = x.astype(jnp.bfloat16)
    rest = x - hi.astype(jnp.float32)
    mid = rest.astype(jnp.bfloat16)
    lo = (rest - mid.astype(jnp.float32)).astype(jnp.bfloat16)
    return hi, mid, lo


def dot(x, y):
    return jnp.dot(x, y, preferred_element_type=jnp.float32)


def pair_table(fine, coarse, shift, transposed):
    shape = (fine, coarse) if not transposed else (coarse, fine)
    f = lax.broadcasted_iota(jnp.int32, shape, 1 if transposed else 0)
    c = lax.broadcasted_iota(jnp.int32, shape, 0 if transposed else 1)
    return (((f + shift) // 2) == c).astype(jnp.float32).astype(jnp.bfloat16)


def face_steps(
    s, q, S, Q, pieces, goal, rhs, parent, fa, rows_buf, part_out, part_in,
    hot_buf, piece_send, piece_recv, ring_send, ring_recv, part_send, part_recv,
):
    NX, NYL, NZL = rhs.shape
    R = NYL // pieces
    tiles_z = NZL // TILE
    holders = ((0, 0, 0), (1, S - 1, NX - 1))

    def piece(face, plane, k):
        return pltpu.make_async_remote_copy(
            src_ref=rhs.at[plane, pl.ds(k * R, R)], dst_ref=fa.at[face, q],
            send_sem=piece_send.at[face, k], recv_sem=piece_recv.at[face],
            device_id=(k, q), device_id_type=MESH,
        )
    def scatter(d):
        face, slab, plane = holders[d]
        for k in range(pieces):
            if k != slab:
                piece(face, plane, k).start()
        if slab < pieces:
            fa[face, q] = rhs[plane, pl.ds(slab * R, R), :]

    def tables():
        local = lax.broadcasted_iota(jnp.int32, (TILE, goal.shape[1]), 0)
        for k in range(S):
            owner = lax.rem(s + k, S) * Q + q
            hot = (goal[...] - owner * TILE) == local
            hot_buf[pl.ds(k * TILE, TILE), :] = hot.astype(jnp.float32).astype(jnp.bfloat16)

    def ring(k):
        return pltpu.make_async_remote_copy(
            src_ref=fa.at[:, q], dst_ref=fa.at[:, q],
            send_sem=ring_send.at[k], recv_sem=ring_recv.at[k],
            device_id=(s, lax.rem(q + k, Q)), device_id_type=MESH,
        )

    def ring_arrival(k):
        source = lax.rem(q + Q - k, Q)
        return pltpu.make_async_remote_copy(
            src_ref=fa.at[:, source], dst_ref=fa.at[:, source],
            send_sem=ring_send.at[k], recv_sem=ring_recv.at[k],
            device_id=(s, source), device_id_type=MESH,
        )

    def part(k):
        return pltpu.make_async_remote_copy(
            src_ref=part_out.at[k], dst_ref=part_in.at[k],
            send_sem=part_send.at[k], recv_sem=part_recv.at[k],
            device_id=(lax.rem(s + k, S), q), device_id_type=MESH,
        )

    def gather():
        @pl.when(s < pieces)
        def _():
            for face, slab, plane in holders:
                @pl.when(s != slab)
                def _():
                    pltpu.make_async_remote_copy(
                        src_ref=fa.at[face, q], dst_ref=fa.at[face, q],
                        send_sem=piece_send.at[face, 0], recv_sem=piece_recv.at[face],
                        device_id=(slab, q), device_id_type=MESH,
                    ).wait_recv()
            for k in range(1, Q):
                ring(k).start()

    def finish():
        @pl.when(s < pieces)
        def _():
            for k in range(1, Q):
                ring_arrival(k).wait_recv()
            for face in range(2):
                for a in range(Q):
                    for b in range(tiles_z):
                        t = (face * Q + a) * tiles_z + b
                        rows_buf[pl.ds(t * R, R), :] = fa[face, a, :, pl.ds(b * TILE, TILE)]
            parts = jnp.concatenate(split3(rows_buf[...]), axis=1)
            group = 4 if S % 4 == 0 else S
            for g in reversed(range(S // group)):
                sums = dot(hot_buf[pl.ds(g * group * TILE, group * TILE), :], parts)
                sums = sums[:, :TILE] + (sums[:, TILE:2 * TILE] + sums[:, 2 * TILE:])
                for k in range(g * group, (g + 1) * group):
                    part_out[k] = sums[(k - g * group) * TILE:(k - g * group + 1) * TILE]
                    if k > 0:
                        part(k).start()

        total = None
        if pieces == S:
            total = part_out[0]
            for k in range(1, S):
                part(k).wait_recv()
                total = total + part_in[k]
            parent[0] = total
        else:
            parent[...] = jnp.zeros_like(parent)

            @pl.when(s < pieces)
            def _():
                parent[0] = part_out[0]
            for k in range(1, S):
                @pl.when(lax.rem(s + S - k, S) < pieces)
                def _():
                    part(k).wait_recv()
                    parent[0] += part_in[k]

        for face, slab, plane in holders:
            @pl.when(s == slab)
            def _():
                for k in range(pieces):
                    if k != slab:
                        piece(face, plane, k).wait_send()

        @pl.when(s < pieces)
        def _():
            for k in range(1, Q):
                ring(k).wait_send()
            for k in range(1, S):
                part(k).wait_send()

    return scatter, tables, gather, finish


def cycle_kernel(
    S, Q, pieces, cot, goal, rhs, parent,
    f0, f1, f2, g3, m0, m1, m2, m3, c0, c1, gc, bm, n0, n1, gm, bf, h0, h1,
    fa, rows_buf, part_out, part_in, hot_buf,
    load_sem, send_sem, recv_sem, piece_send, piece_recv, ring_send, ring_recv, part_send, part_recv,
):
    s, q = lax.axis_index("slab"), lax.axis_index("pencil")
    has = [s > 0, s < S - 1, q > 0, q < Q - 1]
    corners = ((0, 2), (1, 3), (0, 3), (1, 2))
    has += [jnp.logical_and(has[i], has[j]) for i, j in corners]
    side_s, side_q = (lax.max(s - 1, 0), lax.min(s + 1, S - 1)), (lax.max(q - 1, 0), lax.min(q + 1, Q - 1))
    peers = [(side_s[0], q), (side_s[1], q), (s, side_q[0]), (s, side_q[1])]
    peers += [(side_s[i], side_q[j - 2]) for i, j in corners]
    NX, NYL, NZL = cot.shape
    scatter, tables, gather, finish_faces = face_steps(
        s, q, S, Q, pieces, goal, rhs, parent, fa, rows_buf, part_out, part_in,
        hot_buf, piece_send, piece_recv, ring_send, ring_recv, part_send, part_recv)

    load = pltpu.make_async_copy(cot, f0.at[pl.ds(1, NX), pl.ds(EDGE, NYL)], load_sem)
    load.start()

    barrier = pltpu.get_barrier_semaphore()
    for k in range(1, S):
        pl.semaphore_signal(
            barrier, inc=1, device_id=(lax.rem(s + k, S), q), device_id_type=MESH)
    for k in range(1, Q):
        pl.semaphore_signal(
            barrier, inc=1, device_id=(s, lax.rem(q + k, Q)), device_id_type=MESH)
    for d in range(4, 8):
        @pl.when(has[d])
        def _():
            pl.semaphore_signal(barrier, inc=1, device_id=peers[d], device_id_type=MESH)
    pl.semaphore_wait(barrier, S + Q - 2 + sum(h.astype(jnp.int32) for h in has[4:]))

    def sizes(buf):
        return buf.shape[0] - 2, buf.shape[1] - 2 * EDGE, buf.shape[2]

    def wide(buf):
        return buf is gc or buf is gm

    def sides(buf):
        return range(8) if wide(buf) else range(4)

    def chunks(buf, d):
        return CHUNKS if d < 2 and sizes(buf)[0] > 2 else 1

    def regions(buf, c=0, n=1):
        nx, ny, _ = sizes(buf)
        own_x, own_y = pl.ds(1, nx), pl.ds(EDGE + c * (ny // n), ny // n)
        k = EDGE if wide(buf) else 1
        src_x, halo_x = (1, nx), (0, nx + 1)
        src_y = (pl.ds(EDGE, k), pl.ds(EDGE + ny - k, k))
        halo_y = (pl.ds(EDGE - k, k), pl.ds(EDGE + ny, k))
        src = [buf.at[1, own_y], buf.at[nx, own_y], buf.at[own_x, src_y[0]], buf.at[own_x, src_y[1]]]
        halo = [buf.at[0, own_y], buf.at[nx + 1, own_y], buf.at[own_x, halo_y[0]], buf.at[own_x, halo_y[1]]]
        if wide(buf):
            src += [buf.at[src_x[i], src_y[j - 2]] for i, j in corners]
            halo += [buf.at[halo_x[i], halo_y[j - 2]] for i, j in corners]
        return src, halo

    def copy(rnd, buf, d, c):
        src, halo = regions(buf, c, chunks(buf, d))
        return pltpu.make_async_remote_copy(
            src_ref=src[d], dst_ref=halo[d ^ 1],
            send_sem=send_sem.at[rnd, d, c], recv_sem=recv_sem.at[rnd, d ^ 1, c],
            device_id=peers[d], device_id_type=MESH,
        )

    sent = {}

    def start(rnd, buf, d, c=None):
        sent[rnd] = buf

        @pl.when(has[d])
        def _():
            for i in range(chunks(buf, d)) if c is None else (c,):
                copy(rnd, buf, d, i).start()

    def arrive(rnd, buf, d, c=None):
        n = chunks(buf, d)

        @pl.when(has[d])
        def _():
            for i in range(n) if c is None else (c,):
                src, halo = regions(buf, i, n)
                pltpu.make_async_remote_copy(
                    src_ref=src[d ^ 1], dst_ref=halo[d],
                    send_sem=send_sem.at[rnd, d, i], recv_sem=recv_sem.at[rnd, d, i],
                    device_id=peers[d], device_id_type=MESH,
                ).wait_recv()

    def clear(buf):
        _, halo = regions(buf)
        for d in sides(buf):
            @pl.when(jnp.logical_not(has[d]))
            def _():
                halo[d][...] = jnp.zeros(halo[d].shape, jnp.float32)

    def neighbours(buf, x, r0, rows, before=EDGE, after=EDGE):
        z = buf.shape[2]
        first = r0 + EDGE - before
        count = before + rows + after
        big = buf[x, pl.ds(first, count), :]
        v = big[before:before + rows]
        nb = buf[x - 1, pl.ds(first + before, rows), :] + buf[x + 1, pl.ds(first + before, rows), :]
        nb = nb + pltpu.roll(big, 1, 0)[before:before + rows]
        nb = nb + pltpu.roll(big, count - 1, 0)[before:before + rows]
        lane = lax.broadcasted_iota(jnp.int32, (rows, z), 1)
        nb = nb + jnp.where(lane == 0, 0.0, pltpu.roll(v, 1, 1))
        nb = nb + jnp.where(lane == z - 1, 0.0, pltpu.roll(v, z - 1, 1))
        return v, nb

    def plane_op(buf, x_first, x_count, body):
        ny = sizes(buf)[1]
        rows = min(32, ny)
        per = ny // rows

        def step(i, _):
            body(x_first + i // per, pl.multiple_of((i % per) * rows, rows), rows)
            return 0
        lax.fori_loop(0, x_count * per, step, 0)

    def sweep(rnd, buf, finish, out_rnd=None, out=None, edge_first=None, between=None):
        nx, ny, _ = sizes(buf)

        def body(x, r0, rows):
            v, nb = neighbours(buf, x, r0, rows)
            finish(x, r0, rows, v, nb)

        def wait(d, c=None):
            if rnd is not None:
                arrive(rnd, buf, d, c)

        def send(d, c=None):
            if out is not None:
                start(out_rnd, out, d, c)
        if out is not None:
            clear(out)
        wait(2)
        wait(3)
        if edge_first is not None:
            for d, x in ((0, 1), (1, nx)):
                @pl.when(jnp.logical_not(has[d]))
                def _():
                    plane_op(buf, x, 1, body)
                    edge_first(d)
        if nx > 2 and rnd is not None:
            plane_op(buf, 2, nx - 2, body)
        if between is not None:
            between()
        if nx > 2:
            rows = ny // CHUNKS
            for c in range(CHUNKS):
                for d, x in ((0, 1), (1, nx)):
                    if edge_first is not None:
                        @pl.when(has[d])
                        def _():
                            wait(d, c)
                            body(x, c * rows, rows)
                    else:
                        wait(d, c)
                        body(x, c * rows, rows)
                    send(d, c)
            if rnd is None:
                plane_op(buf, 2, nx - 2, body)
        elif nx == 2:
            for d in range(2):
                wait(d)
                plane_op(buf, 1 + d, 1, body)
                send(d)
        else:
            wait(0)
            wait(1)
            plane_op(buf, 1, 1, body)
            send(0)
            send(1)
        if out is not None:
            for d in sides(out):
                if d >= 2:
                    send(d)

    def put(out, x, r0, rows, value):
        out[x, pl.ds(r0 + EDGE, rows), :] = value

    def own(buf, x, r0, rows):
        return buf[x, pl.ds(r0 + EDGE, rows), :]

    def smooth_to(out):
        def finish(x, r0, rows, v, nb):
            put(out, x, r0, rows, (1.0 - W) * v + (W / 6.0) * nb)
        return finish

    def restrict(src, dst):
        x, y, z = sizes(src)
        clear(dst)
        parts = []
        for j in range(x // 2):
            parts += split3(own(src, 2 * j + 1, 0, y) + own(src, 2 * j + 2, 0, y))
        half = dot(jnp.concatenate(parts, axis=0), pair_table(z, z // 2, 0, False))
        sy = pair_table(y, y // 2, 0, True)
        for j in range(x // 2):
            both = half[3 * j * y:(3 * j + 1) * y]
            both = both + (half[(3 * j + 1) * y:(3 * j + 2) * y] + half[(3 * j + 2) * y:(3 * j + 3) * y])
            hi, mid, lo = split3(both)
            put(dst, 1 + j, 0, y // 2, dot(sy, hi) + (dot(sy, mid) + dot(sy, lo)))

    def prolong(src, dst):
        nx, ny, z = sizes(src)
        py = pair_table(2 * ny + 2 * EDGE, ny + 2 * EDGE, EDGE, False)
        pz = pair_table(2 * z, z, 0, True)
        for j in range(nx + 2):
            tall = [dot(py, part).astype(jnp.bfloat16) for part in split3(src[j])]
            n = tall[0].shape[0]
            both = dot(jnp.concatenate(tall, axis=0), pz)
            value = 0.125 * (both[:n] + (both[n:2 * n] + both[2 * n:]))
            dst[2 * j] = value
            dst[2 * j + 1] = value

    def correct(back, old, out, scale):
        nx, ny, _ = sizes(out)

        def body(x, r0, rows, before=EDGE, after=EDGE):
            v, nb = neighbours(back, x + 1, r0, rows, before, after)
            put(out, x, r0, rows, own(old, x, r0, rows) - scale * (6.0 * v - nb))
        clear(out)
        plane_op(out, 1, nx, body)
        for d, x in ((0, 0), (1, nx + 1)):
            @pl.when(has[d])
            def _():
                plane_op(out, x, 1, body)
        for d, r0, before, after in ((2, -EDGE, 0, EDGE), (3, ny, EDGE, 0)):
            @pl.when(has[d])
            def _():
                for x in range(1, nx + 1):
                    body(x, r0, EDGE, before, after)

    def send_all(rnd, buf):
        for d in sides(buf):
            start(rnd, buf, d)

    def arrive_all(rnd, buf):
        for d in sides(buf):
            arrive(rnd, buf, d)

    def send_early(c):
        start(12, g3, 0, c)
        start(12, g3, 1, c)

    clear(f0)
    load.wait()
    send_all(0, f0)
    tables()
    sweep(0, f0, smooth_to(f1), 1, f1)
    sweep(1, f1, smooth_to(f2), 2, f2)
    sweep(2, f2, smooth_to(g3))
    restrict(g3, m0)
    send_all(3, m0)
    send_early(0)
    start(12, g3, 2)
    start(12, g3, 3)
    sweep(3, m0, smooth_to(m1), 4, m1)
    send_early(1)
    sweep(4, m1, smooth_to(m2), 5, m2)
    send_early(2)
    sweep(5, m2, smooth_to(m3))
    restrict(m3, c0)
    send_all(6, c0)
    send_all(9, m3)
    sweep(6, c0, smooth_to(c1), 7, c1)
    send_early(3)

    def coarse_total(x, r0, rows, v, nb):
        value = (1.0 - W) * v + (W / 6.0) * nb
        put(gc, x, r0, rows, coefficient(2) * (own(c0, x, r0, rows) + own(c1, x, r0, rows) + value))
    sweep(7, c1, coarse_total, 8, gc)
    arrive_all(8, gc)
    prolong(gc, bm)
    arrive_all(9, m3)
    correct(bm, m3, n0, 0.25)
    sweep(None, n0, smooth_to(n1), 10, n1)

    def medium_total(x, r0, rows, v, nb):
        value = (1.0 - W) * v + (W / 6.0) * nb
        total = own(m0, x, r0, rows) + own(m1, x, r0, rows) + own(m2, x, r0, rows)
        total = total + own(n0, x, r0, rows) + v + value
        put(gm, x, r0, rows, coefficient(1) * total + own(bm, x + 1, r0, rows))
    sweep(10, n1, medium_total, 11, gm)
    arrive_all(11, gm)
    prolong(gm, bf)
    arrive_all(12, g3)
    correct(bf, g3, h0, 1.0)
    sweep(None, h0, smooth_to(h1), 13, h1)

    def first_terms(x, r0, rows):
        total = own(f0, x, r0, rows) + own(f1, x, r0, rows) + own(f2, x, r0, rows)
        total = total + own(h0, x, r0, rows)
        rhs[x - 1, pl.ds(r0, rows), :] = coefficient(0) * total + own(bf, x + 1, r0, rows)
    plane_op(h0, 1, NX, first_terms)

    def last_terms(x, r0, rows, v, nb):
        value = (1.0 - W) * v + (W / 6.0) * nb
        before = rhs[x - 1, pl.ds(r0, rows), :]
        rhs[x - 1, pl.ds(r0, rows), :] = before + coefficient(0) * (v + value)
    sweep(13, h1, last_terms, edge_first=scatter, between=gather)
    finish_faces()
    for rnd, buf in sent.items():
        for d in sides(buf):
            @pl.when(has[d])
            def _():
                for c in range(chunks(buf, d)):
                    copy(rnd, buf, d, c).wait_send()


def run_cycle(cotangent, seg_rows, owners, offsets):
    S, Q = lax.axis_size("slab"), lax.axis_size("pencil")
    x, y, z = cotangent.shape
    pieces = min(S, y // EDGE)
    R = y // pieces
    targets = source_rows(seg_rows, owners, offsets, TILE)
    first = jnp.minimum(lax.axis_index("slab"), pieces - 1) * R
    goal = lax.dynamic_slice_in_dim(targets, first, R, axis=1).reshape(1, -1)

    def padded(level, deep=1):
        k = 2**level
        return pltpu.VMEM((x // k + 2 * deep, y // k + 2 * EDGE, z // k), jnp.float32)
    scratch = [padded(0)] * 4 + [padded(1)] * 4 + [padded(2)] * 3
    scratch += [padded(1, 2)] + [padded(1)] * 3 + [padded(0, 2)] + [padded(0)] * 2
    scratch += [
        pltpu.VMEM((2, Q, R, z), jnp.float32),
        pltpu.VMEM((goal.shape[1], TILE), jnp.float32),
        pltpu.VMEM((S, TILE, TILE), jnp.float32),
        pltpu.VMEM((S, TILE, TILE), jnp.float32),
        pltpu.VMEM((S * TILE, goal.shape[1]), jnp.bfloat16),
        pltpu.SemaphoreType.DMA,
        pltpu.SemaphoreType.DMA((ROUNDS, 8, CHUNKS)),
        pltpu.SemaphoreType.DMA((ROUNDS, 8, CHUNKS)),
        pltpu.SemaphoreType.DMA((2, pieces)),
        pltpu.SemaphoreType.DMA((2,)),
        pltpu.SemaphoreType.DMA((Q,)),
        pltpu.SemaphoreType.DMA((Q,)),
        pltpu.SemaphoreType.DMA((S,)),
        pltpu.SemaphoreType.DMA((S,)),
    ]
    return pl.pallas_call(
        functools.partial(cycle_kernel, S, Q, pieces),
        out_shape=(
            jax.ShapeDtypeStruct(cotangent.shape, jnp.float32),
            jax.ShapeDtypeStruct((1, TILE, TILE), jnp.float32),
        ),
        in_specs=[pl.BlockSpec(memory_space=pl.ANY), pl.BlockSpec(memory_space=pltpu.VMEM)],
        out_specs=(pl.BlockSpec(memory_space=pltpu.VMEM), pl.BlockSpec(memory_space=pltpu.VMEM)),
        scratch_shapes=scratch,
        compiler_params=pltpu.CompilerParams(
            collective_id=0, has_side_effects=True, vmem_limit_bytes=48 * 2**20
        ),
        name="vcycle",
    )(cotangent, goal)


def source_rows(seg_rows, owners, offsets, tile_size):
    starts = jnp.cumsum(seg_rows, axis=1) - seg_rows
    position = jnp.arange(tile_size, dtype=jnp.int32)[None, None, :]
    inside = (position >= starts[:, :, None]) & (position < (starts + seg_rows)[:, :, None])
    value = owners[:, :, None] * tile_size + offsets[:, :, None] + position - starts[:, :, None]
    return jnp.sum(jnp.where(inside, value, 0), axis=1)


def shards(cotangent, seg_rows, owners, offsets):
    rhs_grad, parent_grad = run_cycle(cotangent, seg_rows, owners, offsets)
    return (rhs_grad, parent_grad)


def solution(mesh):
    return jax.shard_map(
        shards,
        mesh=mesh,
        in_specs=(P("slab", "pencil", None), P(), P(), P()),
        out_specs=(P("slab", "pencil", None), P(("slab", "pencil"), None, None)),
        check_vma=False,
    )
```

time: 92.6 us -> 93.7 us (1.012)
  Pallas kernels: 86.7 us -> 88.2 us
    pallas_call x1, Pallas kernels: 86.7 us -> 88.2 us  [run_cycle(): pl.pallas_call(functools.partial(cycle_kernel, S, Q, pieces), out_shape=(...]
where the time goes in v3:
time: 93.7 us; the launch traced here: 93.4 us
  Pallas kernels  88.2 us (94%)
  local copies, waits for them, and re-layouts  4.35 us (5%)
    pallas_call x1, Pallas kernels, run_cycle(): pl.pallas_call(functools.partial(cycle_kernel, S, Q, pieces), out_shape=(...  88.2 us
    unnamed x10, local copies, waits for them, and re-layouts  4.19 us

profile of v3, /device:TPU:0, one launch (start us, length us, event | category | flops | bytes accessed | tf_op | source)
XLA Modules:
  0.0 93.4 jit_solution(12606760864242337026)
XLA Ops:
  0.6 0.0 copy-start.1
  0.6 0.7 copy-done.1
  1.4 0.0 copy-start.2
  1.4 0.0 copy-start.3
  1.4 0.7 copy-done.2
  2.0 0.0 copy-done.3
  2.1 0.1 select_reduce_fusion
  2.2 0.1 constant_dynamic-slice_fusion
  2.3 0.1 reshape.12.goal
  2.3 0.0 copy-start
  2.3 1.2 %copy-done = f32[4,128,512]{2,1,0:T(8,128)S(1)} copy-done((f32[4,128,512]{2,1,0:T(8,128)S(1)}, f32[4,128,512]{2,1,0:T(8,128)}, u32[]{:S(2)}) %copy-start) | copy-done | bytes 1048600
  3.6 88.2 %vcycle.1 = (f32[4,128,512]{2,1,0:T(8,128)S(1)}, f32[1,128,128]{2,1,0:T(8,128)S(1)}) custom-call(f32[4,128,512]{2,1,0:T(8,128)S(1)} %copy-done, s32[1,512]{1,0:T(1,128)S(1)} %reshape.12.goal), custom_call_target="tpu_custom_call" | custom-call | tf_op jit(solution)/shard_map/vcycle/pallas_call | solution.py:505
  91.8 1.0 %copy.14 = f32[4,128,512]{2,1,0:T(8,128)} copy(f32[4,128,512]{2,1,0:T(8,128)S(1)} %get-tuple-element.4) | data formatting | bytes 2097152
  92.8 0.6 copy.15
  (3 shorter events, 0.0 us)
Async XLA Ops:
  0.6 0.7 copy-start.1
  1.4 0.7 copy-start.2
  1.4 0.7 copy-start.3
  2.3 1.2 %copy-start = (f32[4,128,512]{2,1,0:T(8,128)S(1)}, f32[4,128,512]{2,1,0:T(8,128)}, u32[]{:S(2)}) copy-start(f32[4,128,512]{2,1,0:T(8,128)} %cot.1) | copy-start | bytes 3145732

commit v4 on v3

--- a/solution.py
+++ b/solution.py
@@ -208,7 +208,7 @@
     def regions(buf, c=0, n=1):
         nx, ny, _ = sizes(buf)
         own_x, own_y = pl.ds(1, nx), pl.ds(EDGE + c * (ny // n), ny // n)
-        k = EDGE if wide(buf) else 1
+        k = EDGE
         src_x, halo_x = (1, nx), (0, nx + 1)
         src_y = (pl.ds(EDGE, k), pl.ds(EDGE + ny - k, k))
         halo_y = (pl.ds(EDGE - k, k), pl.ds(EDGE + ny, k))

time: 93.7 us -> 92.8 us (level)
  no operation moved by 1% of the time
where the time goes in v4:
time: 92.8 us; the launch traced here: 92.6 us
  Pallas kernels  87.4 us (94%)
  local copies, waits for them, and re-layouts  4.35 us (5%)
    pallas_call x1, Pallas kernels, run_cycle(): pl.pallas_call(functools.partial(cycle_kernel, S, Q, pieces), out_shape=(...  87.4 us
    unnamed x10, local copies, waits for them, and re-layouts  4.19 us

profile of v4, /device:TPU:0, one launch (start us, length us, event | category | flops | bytes accessed | tf_op | source)
XLA Modules:
  0.0 92.6 jit_solution(5670221375646898019)
XLA Ops:
  0.6 0.0 copy-start.1
  0.6 0.7 copy-done.1
  1.4 0.0 copy-start.2
  1.4 0.0 copy-start.3
  1.4 0.7 copy-done.2
  2.0 0.0 copy-done.3
  2.1 0.1 select_reduce_fusion
  2.2 0.1 constant_dynamic-slice_fusion
  2.3 0.1 reshape.12.goal
  2.3 0.0 copy-start
  2.3 1.2 %copy-done = f32[4,128,512]{2,1,0:T(8,128)S(1)} copy-done((f32[4,128,512]{2,1,0:T(8,128)S(1)}, f32[4,128,512]{2,1,0:T(8,128)}, u32[]{:S(2)}) %copy-start) | copy-done | bytes 1048600
  3.6 87.4 %vcycle.1 = (f32[4,128,512]{2,1,0:T(8,128)S(1)}, f32[1,128,128]{2,1,0:T(8,128)S(1)}) custom-call(f32[4,128,512]{2,1,0:T(8,128)S(1)} %copy-done, s32[1,512]{1,0:T(1,128)S(1)} %reshape.12.goal), custom_call_target="tpu_custom_call" | custom-call | tf_op jit(solution)/shard_map/vcycle/pallas_call | solution.py:505
  91.0 1.0 %copy.14 = f32[4,128,512]{2,1,0:T(8,128)} copy(f32[4,128,512]{2,1,0:T(8,128)S(1)} %get-tuple-element.4) | data formatting | bytes 2097152
  91.9 0.6 copy.15
  (3 shorter events, 0.0 us)
Async XLA Ops:
  0.6 0.7 copy-start.1
  1.4 0.7 copy-start.2
  1.4 0.7 copy-start.3
  2.3 1.2 %copy-start = (f32[4,128,512]{2,1,0:T(8,128)S(1)}, f32[4,128,512]{2,1,0:T(8,128)}, u32[]{:S(2)}) copy-start(f32[4,128,512]{2,1,0:T(8,128)} %cot.1) | copy-start | bytes 3145732

commit v5 on v4

--- a/solution.py
+++ b/solution.py
@@ -221,6 +221,12 @@
 
     def copy(rnd, buf, d, c):
         src, halo = regions(buf, c, chunks(buf, d))
+        if buf is f0:
+            n = NYL // chunks(buf, d)
+            src = (
+                cot.at[0, pl.ds(c * n, n)], cot.at[NX - 1, pl.ds(c * n, n)],
+                cot.at[:, pl.ds(0, EDGE)], cot.at[:, pl.ds(NYL - EDGE, EDGE)],
+            )
         return pltpu.make_async_remote_copy(
             src_ref=src[d], dst_ref=halo[d ^ 1],
             send_sem=send_sem.at[rnd, d, c], recv_sem=recv_sem.at[rnd, d ^ 1, c],
@@ -273,13 +279,13 @@
 
     def plane_op(buf, x_first, x_count, body):
         ny = sizes(buf)[1]
-        rows = min(32, ny)
+        rows = min(16, ny)
         per = ny // rows
 
         def step(i, _):
             body(x_first + i // per, pl.multiple_of((i % per) * rows, rows), rows)
             return 0
-        lax.fori_loop(0, x_count * per, step, 0)
+        lax.fori_loop(0, x_count * per, step, 0, unroll=2)
 
     def sweep(rnd, buf, finish, out_rnd=None, out=None, edge_first=None, between=None):
         nx, ny, _ = sizes(buf)
@@ -287,6 +293,10 @@
         def body(x, r0, rows):
             v, nb = neighbours(buf, x, r0, rows)
             finish(x, r0, rows, v, nb)
+
+        def halves(x, r0, rows):
+            for r in range(r0, r0 + rows, 16):
+                body(x, r, 16)
 
         def wait(d, c=None):
             if rnd is not None:
@@ -317,10 +327,10 @@
                         @pl.when(has[d])
                         def _():
                             wait(d, c)
-                            body(x, c * rows, rows)
+                            halves(x, c * rows, rows)
                     else:
                         wait(d, c)
-                        body(x, c * rows, rows)
+                        halves(x, c * rows, rows)
                     send(d, c)
             if rnd is None:
                 plane_op(buf, 2, nx - 2, body)
@@ -407,10 +417,10 @@
         start(12, g3, 0, c)
         start(12, g3, 1, c)
 
+    send_all(0, f0)
     clear(f0)
+    tables()
     load.wait()
-    send_all(0, f0)
-    tables()
     sweep(0, f0, smooth_to(f1), 1, f1)
     sweep(1, f1, smooth_to(f2), 2, f2)
     sweep(2, f2, smooth_to(g3))
@@ -512,7 +522,7 @@
         out_specs=(pl.BlockSpec(memory_space=pltpu.VMEM), pl.BlockSpec(memory_space=pltpu.VMEM)),
         scratch_shapes=scratch,
         compiler_params=pltpu.CompilerParams(
-            collective_id=0, has_side_effects=True, vmem_limit_bytes=48 * 2**20
+            collective_id=0, has_side_effects=True, vmem_limit_bytes=60 * 2**20
         ),
         name="vcycle",
     )(cotangent, goal)

time: 92.8 us -> 95.2 us (1.026)
  Pallas kernels: 87.4 us -> 89.1 us
    pallas_call x1, Pallas kernels: 87.4 us -> 89.1 us  [run_cycle(): pl.pallas_call(functools.partial(cycle_kernel, S, Q, pieces), out_shape=(...]
where the time goes in v5:
time: 95.2 us; the launch traced here: 94.9 us
  Pallas kernels  89.1 us (94%)
  local copies, waits for them, and re-layouts  5.03 us (5%)
    pallas_call x1, Pallas kernels, run_cycle(): pl.pallas_call(functools.partial(cycle_kernel, S, Q, pieces), out_shape=(...  89.1 us
    unnamed x10, local copies, waits for them, and re-layouts  4.29 us

profile of v5, /device:TPU:0, one launch (start us, length us, event | category | flops | bytes accessed | tf_op | source)
XLA Modules:
  0.0 94.9 jit_solution(11233871362360110455)
XLA Ops:
  0.6 0.0 copy-start.1
  0.6 0.7 copy-done.1
  1.4 0.0 copy-start.2
  1.4 0.0 copy-start.3
  1.4 0.7 copy-done.2
  2.0 0.0 copy-done.3
  2.1 0.1 select_reduce_fusion
  2.2 0.1 constant_dynamic-slice_fusion
  2.3 0.7 reshape.12.goal
  2.9 89.1 %vcycle.1 = (f32[4,128,512]{2,1,0:T(8,128)}, f32[1,128,128]{2,1,0:T(8,128)}) custom-call(f32[4,128,512]{2,1,0:T(8,128)} %cot.1, s32[1,512]{1,0:T(1,128)} %reshape.12.goal), custom_call_target="tpu_custom_call" | custom-call | tf_op jit(solution)/shard_map/vcycle/pallas_call | solution.py:515
  92.0 0.0 copy-start
  92.0 2.3 %copy.14 = f32[4,128,512]{2,1,0:T(8,128)} copy(f32[4,128,512]{2,1,0:T(8,128)} %get-tuple-element.4) | data formatting | bytes 2097152
  94.3 0.0 copy-done
  94.3 0.6 copy.15
  (3 shorter events, 0.0 us)
Async XLA Ops:
  0.6 0.7 copy-start.1
  1.4 0.7 copy-start.2
  1.4 0.7 copy-start.3
  92.0 2.3 %copy-start = (f32[1,128,128]{2,1,0:T(8,128)S(1)}, f32[1,128,128]{2,1,0:T(8,128)}, u32[]{:S(2)}) copy-start(f32[1,128,128]{2,1,0:T(8,128)} %get-tuple-element.5) | copy-start | bytes 196612

commit v6 on v4

--- a/solution.py
+++ b/solution.py
@@ -279,7 +279,7 @@
         def step(i, _):
             body(x_first + i // per, pl.multiple_of((i % per) * rows, rows), rows)
             return 0
-        lax.fori_loop(0, x_count * per, step, 0)
+        lax.fori_loop(0, x_count * per, step, 0, unroll=2)
 
     def sweep(rnd, buf, finish, out_rnd=None, out=None, edge_first=None, between=None):
         nx, ny, _ = sizes(buf)

time: 92.8 us -> 92.1 us (level)
  no operation moved by 1% of the time
where the time goes in v6:
time: 92.1 us; the launch traced here: 91.8 us
  Pallas kernels  86.6 us (94%)
  local copies, waits for them, and re-layouts  4.35 us (5%)
    pallas_call x1, Pallas kernels, run_cycle(): pl.pallas_call(functools.partial(cycle_kernel, S, Q, pieces), out_shape=(...  86.6 us
    unnamed x10, local copies, waits for them, and re-layouts  4.19 us

profile of v6, /device:TPU:0, one launch (start us, length us, event | category | flops | bytes accessed | tf_op | source)
XLA Modules:
  0.0 91.8 jit_solution(9007120496441858314)
XLA Ops:
  0.6 0.0 copy-start.1
  0.6 0.7 copy-done.1
  1.4 0.0 copy-start.2
  1.4 0.0 copy-start.3
  1.4 0.7 copy-done.2
  2.0 0.0 copy-done.3
  2.1 0.1 select_reduce_fusion
  2.2 0.1 constant_dynamic-slice_fusion
  2.3 0.1 reshape.12.goal
  2.3 0.0 copy-start
  2.3 1.2 %copy-done = f32[4,128,512]{2,1,0:T(8,128)S(1)} copy-done((f32[4,128,512]{2,1,0:T(8,128)S(1)}, f32[4,128,512]{2,1,0:T(8,128)}, u32[]{:S(2)}) %copy-start) | copy-done | bytes 1048600
  3.6 86.6 %vcycle.1 = (f32[4,128,512]{2,1,0:T(8,128)S(1)}, f32[1,128,128]{2,1,0:T(8,128)S(1)}) custom-call(f32[4,128,512]{2,1,0:T(8,128)S(1)} %copy-done, s32[1,512]{1,0:T(1,128)S(1)} %reshape.12.goal), custom_call_target="tpu_custom_call" | custom-call | tf_op jit(solution)/shard_map/vcycle/pallas_call | solution.py:505
  90.2 1.0 %copy.14 = f32[4,128,512]{2,1,0:T(8,128)} copy(f32[4,128,512]{2,1,0:T(8,128)S(1)} %get-tuple-element.4) | data formatting | bytes 2097152
  91.2 0.6 copy.15
  (3 shorter events, 0.0 us)
Async XLA Ops:
  0.6 0.7 copy-start.1
  1.4 0.7 copy-start.2
  1.4 0.7 copy-start.3
  2.3 1.2 %copy-start = (f32[4,128,512]{2,1,0:T(8,128)S(1)}, f32[4,128,512]{2,1,0:T(8,128)}, u32[]{:S(2)}) copy-start(f32[4,128,512]{2,1,0:T(8,128)} %cot.1) | copy-start | bytes 3145732
